TPU v7x, 32 devices: a whole 2x2x4 slice. The times are simulated.
32 devices in a mesh: chord: 4 (over y, core), span: 2 (over x), wall: 4 (over z).
Axes of the slice: x: 2, y: 2, z: 4, core: 2. Of those that a mesh axis runs over, the one named last changes fastest.
Arguments:
- sensitivity: float32 [6, 32, 32, 512], P(None, 'chord', 'span', 'wall'), may hold values from -6 to 6
- diagonal: float32 [6, 32, 32, 512], P(None, 'chord', 'span', 'wall'), may hold values from 10 to 20
- face_coef: float32 [3, 32, 32, 512], P(None, 'chord', 'span', 'wall'), may hold values from 0.3 to 1.5
- upper_blocks: float32 [3, 6, 6], replicated, may hold values from -2.5 to 2.5
- lower_blocks: float32 [3, 6, 6], replicated, may hold values from -2.5 to 2.5
- iface_blocks: float32 [2, 6, 6], replicated, may hold values from -2.5 to 2.5
- production: float32 [32, 32, 512], P('chord', 'span', 'wall'), may hold values from -6 to 6
- send_cell: int32 [4, 2, 4, 2, 64], P('chord', 'span', 'wall'), may hold values from 0 to 16383
- target_cell: int32 [4, 2, 4, 2, 64], P('chord', 'span', 'wall'), may hold values from 0 to 16383
- orient: int32 [4, 2, 4, 2, 64], P('chord', 'span', 'wall'), may hold values from 0 to 1
- iface_weight: float32 [4, 2, 4, 2, 64], P('chord', 'span', 'wall'), may hold values from 0.5 to 2
Outputs:
- adjoint: float32 [6, 32, 32, 512], P(None, 'chord', 'span', 'wall')
- gradient: float32 [32, 32, 512], P('chord', 'span', 'wall')
All inputs are finite; a program needn't handle non-finite values.
Results may differ from a plain program's by a relative error of at most 0.0001.
Values sent between devices are 32-bit elements; how exact they have to be, the bound alone decides.
A program may use at most 64 MiB of HBM per device.

v0:
```python
import jax
import jax.numpy as jnp
from jax import lax
from jax.sharding import PartitionSpec as P

SWEEPS = 3


def with_halo(block, sides, width):
    for axis, dim in sides:
        count = lax.axis_size(axis)
        forward = [(i, i + 1) for i in range(count - 1)]
        backward = [(target, source) for source, target in forward]
        low = lax.ppermute(
            lax.slice_in_dim(block, block.shape[dim] - width, None, axis=dim), axis, forward
        )
        high = lax.ppermute(lax.slice_in_dim(block, 0, width, axis=dim), axis, backward)
        block = jnp.concatenate([low, block, high], axis=dim)
    return block


def couple(block, field):
    return jnp.einsum("ji,jxyz->ixyz", block, field, precision=lax.Precision.HIGHEST)


def neighbour_pairs(adjoint):
    padded = with_halo(adjoint, (("chord", 1), ("span", 2), ("wall", 3)), 1)
    return [
        (padded[:, 2:, 1:-1, 1:-1], padded[:, :-2, 1:-1, 1:-1]),
        (padded[:, 1:-1, 2:, 1:-1], padded[:, 1:-1, :-2, 1:-1]),
        (padded[:, 1:-1, 1:-1, 2:], padded[:, 1:-1, 1:-1, :-2]),
    ]


def local(
    sensitivity,
    diagonal,
    face_coef,
    upper_blocks,
    lower_blocks,
    iface_blocks,
    production,
    send_cell,
    target_cell,
    orient,
    iface_weight,
):
    n_span = lax.axis_size("span")
    n_var = sensitivity.shape[0]
    slots = send_cell.shape[-1]
    source_index = send_cell.reshape(-1)
    orient_rows = orient.reshape(1, n_span, slots)
    weight_rows = iface_weight.reshape(1, n_span, slots)
    received_targets = lax.all_to_all(
        target_cell.reshape(n_span, slots), "span", split_axis=0, concat_axis=0, tiled=True
    ).reshape(-1)
    adjoint = sensitivity / diagonal
    for sweep in range(SWEEPS):
        pairs = neighbour_pairs(adjoint)
        applied = diagonal * adjoint
        for axis_num in range(3):
            upper, lower = pairs[axis_num]
            applied = applied + face_coef[axis_num][None] * (
                couple(upper_blocks[axis_num], upper) + couple(lower_blocks[axis_num], lower)
            )
        source = adjoint.reshape(n_var, -1)[:, source_index].reshape(n_var, n_span, slots)
        first = jnp.einsum("ji,jdk->idk", iface_blocks[0], source, precision=lax.Precision.HIGHEST)
        second = jnp.einsum("ji,jdk->idk", iface_blocks[1], source, precision=lax.Precision.HIGHEST)
        outgoing = jnp.where(orient_rows == 1, second, first) * weight_rows
        incoming = lax.all_to_all(outgoing, "span", split_axis=1, concat_axis=1, tiled=True)
        coupled = jnp.zeros(
            (n_var, adjoint.shape[1] * adjoint.shape[2] * adjoint.shape[3]), jnp.float32
        )
        coupled = (
            coupled.at[:, received_targets].add(incoming.reshape(n_var, -1)).reshape(adjoint.shape)
        )
        applied = applied + coupled
        adjoint = adjoint + (sensitivity - applied) / diagonal
    gradient = production * adjoint[n_var - 1]
    return (adjoint, gradient)


def solution(mesh):
    placed = (
        P(None, "chord", "span", "wall"),
        P(None, "chord", "span", "wall"),
        P(None, "chord", "span", "wall"),
        P(),
        P(),
        P(),
        P("chord", "span", "wall"),
        P("chord", "span", "wall", None, None),
        P("chord", "span", "wall", None, None),
        P("chord", "span", "wall", None, None),
        P("chord", "span", "wall", None, None),
    )
    return jax.shard_map(
        local,
        mesh=mesh,
        in_specs=placed,
        out_specs=(P(None, "chord", "span", "wall"), P("chord", "span", "wall")),
        check_vma=False,
    )
```

profile of v0, /device:TPU:0, one launch (start us, length us, event | category | flops | bytes accessed | tf_op | source)
XLA Modules:
  0.0 183.3 jit_solution(6933228111484863361)
XLA Ops:
  0.7 4.3 %all-to-all-start = ((s32[2,1,64]{2,1,0:T(1,128)}), s32[2,1,64]{2,1,0:T(1,128)S(1)}, u32[]{:S(2)}, u32[]{:S(2)}) async-start(s32[2,1,64]{2,1,0:T(1,128)} %bitcast.234), calls=%async_computation | async-start | bytes 2048 | tf_op jit(solution)/shard_map/all_to_all | solution.py:54
  5.0 1.6 copy_divide_fusion
  6.6 1.3 collective-permute-start
  7.9 3.0 %collective-permute-start.1 = (f32[6,1,16,128]{3,0,2,1:T(8,128)S(1)}, f32[6,1,16,128]{3,0,2,1:T(8,128)S(1)}, u32[]{:S(2)}, u32[]{:S(2)}) collective-permute-start(f32[6,1,16,128]{3,0,2,1:T(8,128)S(1)} %get-tuple-element.24), channel_id=1, source_target_pairs={{0,8},{8,16},{16,24},{1,9},{9,17},{17,25},{2,10},{10,18},{18,26},{... | collective-permute-start | bytes 147464 | tf_op jit(solution)/shard_map/ppermute | solution.py:14
  11.0 5.3 %copy.130 = f32[6,16384]{0,1:T(8,128)} copy(f32[6,16384]{1,0:T(8,128)S(1)} %bitcast.212) | data formatting | bytes 786432 | tf_op jit(solution)/shard_map/reshape | solution.py:66
  17.1 4.0 %gather_fusion = f32[128,6]{1,0:T(8,128)S(1)} fusion(f32[6,16384]{0,1:T(8,128)} %copy.130, s32[1024]{0:T(1024)S(1)} %pad_clamp_fusion), kind=kCustom, calls=%fused_computation | custom fusion | bytes 6656 | tf_op jit(solution)/shard_map/gather | solution.py:66
  22.4 3.3 %all-to-all-start.1 = ((f32[2,1,384]{2,1,0:T(1,128)}), f32[2,1,384]{2,1,0:T(1,128)S(1)}, u32[]{:S(2)}, u32[]{:S(2)}) async-start(f32[2,1,384]{2,1,0:T(1,128)} %reshape.220), calls=%async_computation.1 | async-start | bytes 6144 | tf_op jit(solution)/shard_map/all_to_all | solution.py:70
  26.9 2.6 %all-to-all-done.1 = f32[2,1,384]{2,1,0:T(1,128)S(1)} async-done(((f32[2,1,384]{2,1,0:T(1,128)}), f32[2,1,384]{2,1,0:T(1,128)S(1)}, u32[]{:S(2)}, u32[]{:S(2)}) %all-to-all-start.1) | async-done | bytes 3104 | tf_op jit(solution)/shard_map/all_to_all | solution.py:70
  30.9 4.8 %scatter_custom_fusion = f32[6,16384]{0,1:T(8,128)} fusion(s32[128]{0:T(128)S(1)} %fusion.165, f32[128,6]{1,0:T(8,128)S(1)} %copy.138, f32[]{:T(128)} %constant.0.clone.1), kind=kCustom, calls=%fused_computation.10 | custom fusion | flops 768 | bytes 393220 | tf_op jit(solution)/shard_map/scatter-add | solution.py:75
  35.6 5.9 %copy.140 = f32[6,8,16,128]{3,0,2,1:T(8,128)} copy(f32[6,8,16,128]{0,3,2,1:T(8,128)} %bitcast.216) | data formatting | bytes 786432 | tf_op jit(solution)/shard_map/reshape | solution.py:75
  41.6 1.3 collective-permute-start.2
  42.9 4.7 %collective-permute-start.3 = (f32[6,10,1,128]{3,0,2,1:T(8,128)S(1)}, f32[6,10,1,128]{3,0,2,1:T(8,128)S(1)}, u32[]{:S(2)}, u32[]{:S(2)}) collective-permute-start(f32[6,10,1,128]{3,0,2,1:T(8,128)S(1)} %get-tuple-element.18), channel_id=1, source_target_pairs={{0,4},{1,5},{2,6},{3,7},{8,12},{9,13},{10,14},{11,15},{16,20},{17,... | collective-permute-start | bytes 92168 | tf_op jit(solution)/shard_map/ppermute | solution.py:14
  47.6 1.3 fusion.99
  48.9 2.3 %fusion.26 = f32[6,8,16,128]{3,0,2,1:T(8,128)} fusion(f32[8,16,128,6]{2,3,1,0:T(8,128)S(1)} %fusion.99, f32[6,1,16,128]{3,0,2,1:T(8,128)S(1)} %collective-permute-done, f32[6,8,16,128]{3,0,2,1:T(8,128)S(1)} %copy_divide_fusion, f32[6,8,16,128]{3,2,1,0:T(8,128)S(1)} %copy-done, f32[8,16,128]{2,1,0:T(8,128)S(1)} %get-tuple-element.27, f32[3,6,6]{2,1,0:T(8,128)} %param.14), kind=kOutput, calls=%fused_computation.38 | convolution fusion | flops 7581696 | bytes 2494464 | tf_op jit(solution)/shard_map/ji,jxyz->ixyz/dot_general | solution.py:23
  52.7 3.9 %collective-permute-start.5 = (f32[6,10,18,1]{2,3,1,0:T(1,128)S(1)}, f32[6,10,18,1]{2,3,1,0:T(1,128)S(1)}, u32[]{:S(2)}, u32[]{:S(2)}) collective-permute-start(f32[6,10,18,1]{2,3,1,0:T(1,128)S(1)} %copy.126), channel_id=1, source_target_pairs={{0,1},{1,2},{2,3},{4,5},{5,6},{6,7},{8,9},{9,10},{10,11},{12,13},{... | collective-permute-start | bytes 12968 | tf_op jit(solution)/shard_map/ppermute | solution.py:14
  58.4 1.4 fusion.58
  60.3 1.4 fusion.123
  63.4 1.8 fusion.32
  65.2 2.3 %fusion.36 = f32[6,8,16,128]{3,0,2,1:T(8,128)S(1)} fusion(f32[6,8,16,128]{3,0,2,1:T(8,128)S(1)} %copy_divide_fusion, f32[6,8,16,128]{3,0,2,1:T(8,128)} %copy.140, f32[6,8,16,128]{3,0,2,1:T(8,128)S(1)} %fusion.32, f32[6,8,16,128]{3,0,2,1:T(8,128)} %fusion.26, f32[8,16,128,6]{2,3,1,0:T(8,128)S(1)} %fusion.58, f32[6,8,16,128]{3,2,1,0:T(8,128)S(1)} %copy-done, ...), kind=kOutput, calls=%fused_computation.51 | convolution fusion | flops 8256000 | bytes 4567040 | tf_op jit(solution)/shard_map/ji,jxyz->ixyz/dot_general | solution.py:23
  67.6 5.3 %copy.154 = f32[6,16384]{0,1:T(8,128)} copy(f32[6,16384]{1,0:T(8,128)S(1)} %bitcast.214) | data formatting | bytes 786432 | tf_op jit(solution)/shard_map/reshape | solution.py:66
  72.9 4.1 %gather_fusion.1 = f32[128,6]{1,0:T(8,128)S(1)} fusion(f32[6,16384]{0,1:T(8,128)} %copy.154, s32[1024]{0:T(1024)} %copy-done.14), kind=kCustom, calls=%fused_computation.1 | custom fusion | bytes 6656 | tf_op jit(solution)/shard_map/gather | solution.py:66
  77.2 1.3 collective-permute-start.6
  78.6 3.0 %collective-permute-start.7 = (f32[6,1,16,128]{3,0,2,1:T(8,128)S(1)}, f32[6,1,16,128]{3,0,2,1:T(8,128)S(1)}, u32[]{:S(2)}, u32[]{:S(2)}) collective-permute-start(f32[6,1,16,128]{3,0,2,1:T(8,128)S(1)} %get-tuple-element.22), channel_id=1, source_target_pairs={{0,8},{8,16},{16,24},{1,9},{9,17},{17,25},{2,10},{10,18},{18,26},{... | collective-permute-start | bytes 147464 | tf_op jit(solution)/shard_map/ppermute | solution.py:14
  82.0 6.2 %all_to_all.24 = f32[2,1,384]{2,1,0:T(1,128)S(1)} all-to-all(f32[2,1,384]{2,1,0:T(1,128)S(1)} %reshape.222), channel_id=1, replica_groups=mesh['chord'=4,'span'=2,'wall'=4] {'span'}, dimensions={0} | all-to-all | bytes 6144 | tf_op jit(solution)/shard_map/all_to_all | solution.py:70
  89.0 4.9 %scatter_custom_fusion.1 = f32[6,16384]{0,1:T(8,128)} fusion(s32[128]{0:T(128)} %copy-done.21, f32[128,6]{1,0:T(8,128)S(1)} %copy.160, f32[]{:T(128)} %constant.0.clone.1), kind=kCustom, calls=%fused_computation.8 | custom fusion | flops 768 | bytes 393728 | tf_op jit(solution)/shard_map/scatter-add | solution.py:75
  93.9 5.9 %copy.162 = f32[6,8,16,128]{3,0,2,1:T(8,128)} copy(f32[6,8,16,128]{0,3,2,1:T(8,128)} %bitcast.217) | data formatting | bytes 786432 | tf_op jit(solution)/shard_map/reshape | solution.py:75
  101.2 4.5 %collective-permute-start.9 = (f32[6,10,1,128]{3,0,2,1:T(8,128)S(1)}, f32[6,10,1,128]{3,0,2,1:T(8,128)S(1)}, u32[]{:S(2)}, u32[]{:S(2)}) collective-permute-start(f32[6,10,1,128]{3,0,2,1:T(8,128)S(1)} %get-tuple-element.16), channel_id=1, source_target_pairs={{0,4},{1,5},{2,6},{3,7},{8,12},{9,13},{10,14},{11,15},{16,20},{17,... | collective-permute-start | bytes 92168 | tf_op jit(solution)/shard_map/ppermute | solution.py:14
  106.4 2.3 %fusion.19 = f32[6,8,16,128]{3,0,2,1:T(8,128)} fusion(f32[8,16,128,6]{2,3,1,0:T(8,128)S(1)} %fusion.106, f32[6,1,16,128]{3,0,2,1:T(8,128)S(1)} %collective-permute-done.6, f32[6,8,16,128]{3,0,2,1:T(8,128)S(1)} %fusion.36, f32[6,8,16,128]{3,2,1,0:T(8,128)S(1)} %copy-done, f32[8,16,128]{2,1,0:T(8,128)S(1)} %copy-done.3, f32[3,6,6]{2,1,0:T(8,128)} %param.14), kind=kOutput, calls=%fused_computation.29 | convolution fusion | flops 7581696 | bytes 2494464 | tf_op jit(solution)/shard_map/ji,jxyz->ixyz/dot_general | solution.py:23
  109.5 3.5 %collective-permute-start.11 = (f32[6,10,18,1]{2,3,1,0:T(1,128)S(1)}, f32[6,10,18,1]{2,3,1,0:T(1,128)S(1)}, u32[]{:S(2)}, u32[]{:S(2)}) collective-permute-start(f32[6,10,18,1]{2,3,1,0:T(1,128)S(1)} %copy.151), channel_id=1, source_target_pairs={{0,1},{1,2},{2,3},{4,5},{5,6},{6,7},{8,9},{9,10},{10,11},{12,13},{... | collective-permute-start | bytes 12968 | tf_op jit(solution)/shard_map/ppermute | solution.py:14
  116.0 1.4 fusion.120
  117.4 1.8 collective-permute-done.10
  119.8 1.8 fusion.30
  121.6 2.3 %fusion.40 = f32[6,8,16,128]{3,0,2,1:T(8,128)S(1)} fusion(f32[6,8,16,128]{3,0,2,1:T(8,128)S(1)} %fusion.36, f32[6,8,16,128]{3,0,2,1:T(8,128)} %copy.162, f32[6,8,16,128]{3,0,2,1:T(8,128)S(1)} %fusion.30, f32[6,8,16,128]{3,0,2,1:T(8,128)} %fusion.19, f32[8,16,128,6]{2,3,1,0:T(8,128)S(1)} %fusion.73, f32[6,8,16,128]{3,2,1,0:T(8,128)S(1)} %copy-done, ...), kind=kOutput, calls=%fused_computation.55 | convolution fusion | flops 8256000 | bytes 4567040 | tf_op jit(solution)/shard_map/ji,jxyz->ixyz/dot_general | solution.py:23
  123.9 5.3 %copy.176 = f32[6,16384]{0,1:T(8,128)} copy(f32[6,16384]{1,0:T(8,128)S(1)} %bitcast.213) | data formatting | bytes 786432 | tf_op jit(solution)/shard_map/reshape | solution.py:66
  129.3 4.1 %gather_fusion.2 = f32[128,6]{1,0:T(8,128)S(1)} fusion(f32[6,16384]{0,1:T(8,128)} %copy.176, s32[1024]{0:T(1024)} %copy-done.14), kind=kCustom, calls=%fused_computation.2 | custom fusion | bytes 6656 | tf_op jit(solution)/shard_map/gather | solution.py:66
  133.6 1.3 collective-permute-start.12
  135.0 3.0 %collective-permute-start.13 = (f32[6,1,16,128]{3,0,2,1:T(8,128)S(1)}, f32[6,1,16,128]{3,0,2,1:T(8,128)S(1)}, u32[]{:S(2)}, u32[]{:S(2)}) collective-permute-start(f32[6,1,16,128]{3,0,2,1:T(8,128)S(1)} %get-tuple-element.20), channel_id=1, source_target_pairs={{0,8},{8,16},{16,24},{1,9},{9,17},{17,25},{2,10},{10,18},{18,26},{... | collective-permute-start | bytes 147464 | tf_op jit(solution)/shard_map/ppermute | solution.py:14
  138.4 6.2 %all_to_all.25 = f32[2,1,384]{2,1,0:T(1,128)S(1)} all-to-all(f32[2,1,384]{2,1,0:T(1,128)S(1)} %reshape.224), channel_id=1, replica_groups=mesh['chord'=4,'span'=2,'wall'=4] {'span'}, dimensions={0} | all-to-all | bytes 6144 | tf_op jit(solution)/shard_map/all_to_all | solution.py:70
  145.4 4.9 %scatter_custom_fusion.2 = f32[6,16384]{0,1:T(8,128)} fusion(s32[128]{0:T(128)} %copy-done.21, f32[128,6]{1,0:T(8,128)S(1)} %copy.182, f32[]{:T(128)} %constant.0.clone.1), kind=kCustom, calls=%fused_computation.6 | custom fusion | flops 768 | bytes 393728 | tf_op jit(solution)/shard_map/scatter-add | solution.py:75
  150.3 5.2 %copy.184 = f32[6,8,16,128]{3,0,2,1:T(8,128)S(1)} copy(f32[6,8,16,128]{0,3,2,1:T(8,128)} %bitcast.215) | data formatting | bytes 786432 | tf_op jit(solution)/shard_map/reshape | solution.py:75
  156.8 4.8 %collective-permute-start.15 = (f32[6,10,1,128]{3,0,2,1:T(8,128)S(1)}, f32[6,10,1,128]{3,0,2,1:T(8,128)S(1)}, u32[]{:S(2)}, u32[]{:S(2)}) collective-permute-start(f32[6,10,1,128]{3,0,2,1:T(8,128)S(1)} %get-tuple-element.14), channel_id=1, source_target_pairs={{0,4},{1,5},{2,6},{3,7},{8,12},{9,13},{10,14},{11,15},{16,20},{17,... | collective-permute-start | bytes 92168 | tf_op jit(solution)/shard_map/ppermute | solution.py:14
  161.6 1.3 fusion.113
  162.9 2.3 %fusion.12 = f32[6,8,16,128]{3,0,2,1:T(8,128)} fusion(f32[8,16,128,6]{2,3,1,0:T(8,128)S(1)} %fusion.113, f32[6,1,16,128]{3,0,2,1:T(8,128)S(1)} %collective-permute-done.12, f32[6,8,16,128]{3,0,2,1:T(8,128)S(1)} %fusion.40, f32[6,8,16,128]{3,2,1,0:T(8,128)S(1)} %copy-done, f32[8,16,128]{2,1,0:T(8,128)S(1)} %copy-done.4, f32[3,6,6]{2,1,0:T(8,128)} %param.14), kind=kOutput, calls=%fused_computation.20 | convolution fusion | flops 7581696 | bytes 2494464 | tf_op jit(solution)/shard_map/ji,jxyz->ixyz/dot_general | solution.py:23
  167.3 3.6 %collective-permute-start.17 = (f32[6,10,18,1]{2,3,1,0:T(1,128)}, f32[6,10,18,1]{2,3,1,0:T(1,128)S(1)}, u32[]{:S(2)}, u32[]{:S(2)}) collective-permute-start(f32[6,10,18,1]{2,3,1,0:T(1,128)} %copy.173), channel_id=1, source_target_pairs={{0,1},{1,2},{2,3},{4,5},{5,6},{6,7},{8,9},{9,10},{10,11},{12,13},{... | collective-permute-start | bytes 12968 | tf_op jit(solution)/shard_map/ppermute | solution.py:14
  172.6 2.2 %fusion.88 = f32[8,16,128,6]{2,3,1,0:T(8,128)} fusion(f32[6,1,16,128]{3,0,2,1:T(8,128)S(1)} %collective-permute-done.12, f32[6,8,16,128]{3,0,2,1:T(8,128)S(1)} %fusion.40, f32[6,1,16,128]{3,0,2,1:T(8,128)S(1)} %collective-permute-done.13, f32[6,10,1,128]{3,0,2,1:T(8,128)} %copy-done.5, f32[3,6,6]{2,1,0:T(8,128)} %param.15), kind=kOutput, calls=%fused_computation.113 | convolution fusion | flops 7469568 | bytes 929792 | tf_op jit(solution)/shard_map/ji,jxyz->ixyz/dot_general | solution.py:23
  175.4 1.4 fusion.117
  177.7 1.7 fusion.28
  179.5 2.3 %fusion.44 = f32[6,8,16,128]{3,0,2,1:T(8,128)S(1)} fusion(f32[6,8,16,128]{3,0,2,1:T(8,128)S(1)} %fusion.40, f32[6,8,16,128]{3,0,2,1:T(8,128)S(1)} %copy.184, f32[6,8,16,128]{3,0,2,1:T(8,128)S(1)} %fusion.28, f32[6,8,16,128]{3,0,2,1:T(8,128)} %fusion.12, f32[8,16,128,6]{2,3,1,0:T(8,128)} %fusion.88, f32[6,8,16,128]{3,2,1,0:T(8,128)S(1)} %copy-done, ...), kind=kOutput, calls=%fused_computation.59 | convolution fusion | flops 8256000 | bytes 4567040 | tf_op jit(solution)/shard_map/ji,jxyz->ixyz/dot_general | solution.py:23
  (131 shorter events, 27.3 us)
Async XLA Ops:
  0.6 15.6 %copy-start.19 = (s32[1,1,1,2,64]{4,3,2,1,0:T(2,128)S(1)}, s32[1,1,1,2,64]{4,3,2,1,0:T(2,128)}, u32[]{:S(2)}) copy-start(s32[1,1,1,2,64]{4,3,2,1,0:T(2,128)} %param.18) | copy-start | bytes 1540
  0.6 15.7 %copy-start.15 = (f32[2,6,6]{2,0,1:T(2,128)S(1)}, f32[2,6,6]{2,0,1:T(2,128)}, u32[]{:S(2)}) copy-start(f32[2,6,6]{2,0,1:T(2,128)} %param.16) | copy-start | bytes 868
  0.7 15.8 %copy-start.20 = (s32[1,1,1,2,64]{4,3,2,1,0:T(2,128)S(1)}, s32[1,1,1,2,64]{4,3,2,1,0:T(2,128)}, u32[]{:S(2)}) copy-start(s32[1,1,1,2,64]{4,3,2,1,0:T(2,128)} %param.20) | copy-start | bytes 1540
  0.7 15.8 %copy-start.8 = (f32[3,8,16,128]{3,2,1,0:T(8,128)S(1)}, f32[3,8,16,128]{3,2,1,0:T(8,128)}, u32[]{:S(2)}) copy-start(f32[3,8,16,128]{3,2,1,0:T(8,128)} %param.13) | copy-start | bytes 589828
  0.7 20.7 %copy-start.11 = (f32[1,1,1,2,64]{4,3,2,1,0:T(2,128)S(1)}, f32[1,1,1,2,64]{4,3,2,1,0:T(2,128)}, u32[]{:S(2)}) copy-start(f32[1,1,1,2,64]{4,3,2,1,0:T(2,128)} %param.21) | copy-start | bytes 1540
  0.7 21.7 %all-to-all-start = ((s32[2,1,64]{2,1,0:T(1,128)}), s32[2,1,64]{2,1,0:T(1,128)S(1)}, u32[]{:S(2)}, u32[]{:S(2)}) async-start(s32[2,1,64]{2,1,0:T(1,128)} %bitcast.234), calls=%async_computation | async-start | bytes 2048 | tf_op jit(solution)/shard_map/all_to_all | solution.py:54
  6.6 35.0 %collective-permute-start = (f32[6,1,16,128]{3,0,2,1:T(8,128)S(1)}, f32[6,1,16,128]{3,0,2,1:T(8,128)S(1)}, u32[]{:S(2)}, u32[]{:S(2)}) collective-permute-start(f32[6,1,16,128]{3,0,2,1:T(8,128)S(1)} %get-tuple-element.25), channel_id=1, source_target_pairs={{8,0},{16,8},{24,16},{9,1},{17,9},{25,17},{10,2},{18,10},{26,18},{... | collective-permute-start | bytes 147464 | tf_op jit(solution)/shard_map/ppermute | solution.py:17
  7.9 33.7 %collective-permute-start.1 = (f32[6,1,16,128]{3,0,2,1:T(8,128)S(1)}, f32[6,1,16,128]{3,0,2,1:T(8,128)S(1)}, u32[]{:S(2)}, u32[]{:S(2)}) collective-permute-start(f32[6,1,16,128]{3,0,2,1:T(8,128)S(1)} %get-tuple-element.24), channel_id=1, source_target_pairs={{0,8},{8,16},{16,24},{1,9},{9,17},{17,25},{2,10},{10,18},{18,26},{... | collective-permute-start | bytes 147464 | tf_op jit(solution)/shard_map/ppermute | solution.py:14
  16.4 4.8 %copy-start.14 = (s32[1024]{0:T(1024)}, s32[1024]{0:T(1024)S(1)}, u32[]{:S(2)}) copy-start(s32[1024]{0:T(1024)S(1)} %pad_clamp_fusion) | copy-start | bytes 12292
  16.4 25.1 %copy-start.16 = (pred[2,64]{1,0:T(4,128)(4,1)}, pred[2,64]{1,0:T(4,128)(4,1)S(1)}, u32[]{:S(2)}) copy-start(pred[2,64]{1,0:T(4,128)(4,1)S(1)} %compare_bitcast_fusion) | copy-start | bytes 388
  17.1 31.8 %copy-start.2 = (f32[8,16,128]{2,1,0:T(8,128)}, f32[8,16,128]{2,1,0:T(8,128)S(1)}, u32[]{:S(2)}) copy-start(f32[8,16,128]{2,1,0:T(8,128)S(1)} %get-tuple-element.27) | copy-start | bytes 196612
  22.4 7.1 %all-to-all-start.1 = ((f32[2,1,384]{2,1,0:T(1,128)}), f32[2,1,384]{2,1,0:T(1,128)S(1)}, u32[]{:S(2)}, u32[]{:S(2)}) async-start(f32[2,1,384]{2,1,0:T(1,128)} %reshape.220), calls=%async_computation.1 | async-start | bytes 6144 | tf_op jit(solution)/shard_map/all_to_all | solution.py:70
  26.9 14.7 %copy-start.21 = (s32[128]{0:T(128)}, s32[128]{0:T(128)S(1)}, u32[]{:S(2)}) copy-start(s32[128]{0:T(128)S(1)} %fusion.165) | copy-start | bytes 1540
  30.9 18.1 %copy-start = (f32[6,8,16,128]{3,2,1,0:T(8,128)S(1)}, f32[6,8,16,128]{3,2,1,0:T(8,128)}, u32[]{:S(2)}) copy-start(f32[6,8,16,128]{3,2,1,0:T(8,128)} %param.12) | copy-start | bytes 1179652
  41.6 9.6 %collective-permute-start.2 = (f32[6,10,1,128]{3,0,2,1:T(8,128)S(1)}, f32[6,10,1,128]{3,0,2,1:T(8,128)S(1)}, u32[]{:S(2)}, u32[]{:S(2)}) collective-permute-start(f32[6,10,1,128]{3,0,2,1:T(8,128)S(1)} %get-tuple-element.19), channel_id=1, source_target_pairs={{4,0},{5,1},{6,2},{7,3},{12,8},{13,9},{14,10},{15,11},{20,16},{21,... | collective-permute-start | bytes 92168 | tf_op jit(solution)/shard_map/ppermute | solution.py:17
  42.9 22.3 %copy-start.1 = (f32[6,8,16,128]{3,2,1,0:T(8,128)S(1)}, f32[6,8,16,128]{3,2,1,0:T(8,128)}, u32[]{:S(2)}) copy-start(f32[6,8,16,128]{3,2,1,0:T(8,128)} %param.11) | copy-start | bytes 1179652
  42.9 8.3 %collective-permute-start.3 = (f32[6,10,1,128]{3,0,2,1:T(8,128)S(1)}, f32[6,10,1,128]{3,0,2,1:T(8,128)S(1)}, u32[]{:S(2)}, u32[]{:S(2)}) collective-permute-start(f32[6,10,1,128]{3,0,2,1:T(8,128)S(1)} %get-tuple-element.18), channel_id=1, source_target_pairs={{0,4},{1,5},{2,6},{3,7},{8,12},{9,13},{10,14},{11,15},{16,20},{17,... | collective-permute-start | bytes 92168 | tf_op jit(solution)/shard_map/ppermute | solution.py:14
  51.3 0.6 copy-start.6
  52.7 7.1 %collective-permute-start.5 = (f32[6,10,18,1]{2,3,1,0:T(1,128)S(1)}, f32[6,10,18,1]{2,3,1,0:T(1,128)S(1)}, u32[]{:S(2)}, u32[]{:S(2)}) collective-permute-start(f32[6,10,18,1]{2,3,1,0:T(1,128)S(1)} %copy.126), channel_id=1, source_target_pairs={{0,1},{1,2},{2,3},{4,5},{5,6},{6,7},{8,9},{9,10},{10,11},{12,13},{... | collective-permute-start | bytes 12968 | tf_op jit(solution)/shard_map/ppermute | solution.py:14
  57.1 5.8 %collective-permute-start.4 = (f32[6,10,18,1]{2,3,1,0:T(1,128)S(1)}, f32[6,10,18,1]{2,3,1,0:T(1,128)S(1)}, u32[]{:S(2)}, u32[]{:S(2)}) collective-permute-start(f32[6,10,18,1]{2,3,1,0:T(1,128)S(1)} %copy.123), channel_id=1, source_target_pairs={{1,0},{2,1},{3,2},{5,4},{6,5},{7,6},{9,8},{10,9},{11,10},{13,12},{... | collective-permute-start | bytes 12968 | tf_op jit(solution)/shard_map/ppermute | solution.py:17
  63.4 18.2 %copy-start.12 = (f32[1,1,1,2,64]{4,3,2,1,0:T(2,128)S(1)}, f32[1,1,1,2,64]{4,3,2,1,0:T(2,128)}, u32[]{:S(2)}) copy-start(f32[1,1,1,2,64]{4,3,2,1,0:T(2,128)} %param.21) | copy-start | bytes 1540
  63.4 18.2 %copy-start.17 = (pred[2,64]{1,0:T(4,128)(4,1)S(1)}, pred[2,64]{1,0:T(4,128)(4,1)}, u32[]{:S(2)}) copy-start(pred[2,64]{1,0:T(4,128)(4,1)} %copy-done.16) | copy-start | bytes 388
  77.2 22.6 %collective-permute-start.6 = (f32[6,1,16,128]{3,0,2,1:T(8,128)S(1)}, f32[6,1,16,128]{3,0,2,1:T(8,128)S(1)}, u32[]{:S(2)}, u32[]{:S(2)}) collective-permute-start(f32[6,1,16,128]{3,0,2,1:T(8,128)S(1)} %get-tuple-element.23), channel_id=1, source_target_pairs={{8,0},{16,8},{24,16},{9,1},{17,9},{25,17},{10,2},{18,10},{26,18},{... | collective-permute-start | bytes 147464 | tf_op jit(solution)/shard_map/ppermute | solution.py:17
  78.6 21.3 %collective-permute-start.7 = (f32[6,1,16,128]{3,0,2,1:T(8,128)S(1)}, f32[6,1,16,128]{3,0,2,1:T(8,128)S(1)}, u32[]{:S(2)}, u32[]{:S(2)}) collective-permute-start(f32[6,1,16,128]{3,0,2,1:T(8,128)S(1)} %get-tuple-element.22), channel_id=1, source_target_pairs={{0,8},{8,16},{16,24},{1,9},{9,17},{17,25},{2,10},{10,18},{18,26},{... | collective-permute-start | bytes 147464 | tf_op jit(solution)/shard_map/ppermute | solution.py:14
  89.0 16.7 %copy-start.9 = (f32[3,6,6]{2,1,0:T(8,128)S(1)}, f32[3,6,6]{2,1,0:T(8,128)}, u32[]{:S(2)}) copy-start(f32[3,6,6]{2,1,0:T(8,128)} %param.15) | copy-start | bytes 1300
  89.0 17.4 %copy-start.3 = (f32[8,16,128]{2,1,0:T(8,128)S(1)}, f32[8,16,128]{2,1,0:T(8,128)}, u32[]{:S(2)}) copy-start(f32[8,16,128]{2,1,0:T(8,128)} %copy-done.2) | copy-start | bytes 196612
  99.9 8.8 %collective-permute-start.8 = (f32[6,10,1,128]{3,0,2,1:T(8,128)S(1)}, f32[6,10,1,128]{3,0,2,1:T(8,128)S(1)}, u32[]{:S(2)}, u32[]{:S(2)}) collective-permute-start(f32[6,10,1,128]{3,0,2,1:T(8,128)S(1)} %get-tuple-element.17), channel_id=1, source_target_pairs={{4,0},{5,1},{6,2},{7,3},{12,8},{13,9},{14,10},{15,11},{20,16},{21,... | collective-permute-start | bytes 92168 | tf_op jit(solution)/shard_map/ppermute | solution.py:17
  101.2 7.5 %collective-permute-start.9 = (f32[6,10,1,128]{3,0,2,1:T(8,128)S(1)}, f32[6,10,1,128]{3,0,2,1:T(8,128)S(1)}, u32[]{:S(2)}, u32[]{:S(2)}) collective-permute-start(f32[6,10,1,128]{3,0,2,1:T(8,128)S(1)} %get-tuple-element.16), channel_id=1, source_target_pairs={{0,4},{1,5},{2,6},{3,7},{8,12},{9,13},{10,14},{11,15},{16,20},{17,... | collective-permute-start | bytes 92168 | tf_op jit(solution)/shard_map/ppermute | solution.py:14
  108.7 6.7 %copy-start.7 = (f32[6,10,1,128]{3,0,2,1:T(8,128)}, f32[6,10,1,128]{3,0,2,1:T(8,128)S(1)}, u32[]{:S(2)}) copy-start(f32[6,10,1,128]{3,0,2,1:T(8,128)S(1)} %collective-permute-done.9) | copy-start | bytes 92164
  109.5 5.9 %collective-permute-start.11 = (f32[6,10,18,1]{2,3,1,0:T(1,128)S(1)}, f32[6,10,18,1]{2,3,1,0:T(1,128)S(1)}, u32[]{:S(2)}, u32[]{:S(2)}) collective-permute-start(f32[6,10,18,1]{2,3,1,0:T(1,128)S(1)} %copy.151), channel_id=1, source_target_pairs={{0,1},{1,2},{2,3},{4,5},{5,6},{6,7},{8,9},{9,10},{10,11},{12,13},{... | collective-permute-start | bytes 12968 | tf_op jit(solution)/shard_map/ppermute | solution.py:14
  113.5 5.8 %collective-permute-start.10 = (f32[6,10,18,1]{2,3,1,0:T(1,128)S(1)}, f32[6,10,18,1]{2,3,1,0:T(1,128)S(1)}, u32[]{:S(2)}, u32[]{:S(2)}) collective-permute-start(f32[6,10,18,1]{2,3,1,0:T(1,128)S(1)} %copy.148), channel_id=1, source_target_pairs={{1,0},{2,1},{3,2},{5,4},{6,5},{7,6},{9,8},{10,9},{11,10},{13,12},{... | collective-permute-start | bytes 12968 | tf_op jit(solution)/shard_map/ppermute | solution.py:17
  119.8 18.2 %copy-start.13 = (f32[1,1,1,2,64]{4,3,2,1,0:T(2,128)S(1)}, f32[1,1,1,2,64]{4,3,2,1,0:T(2,128)}, u32[]{:S(2)}) copy-start(f32[1,1,1,2,64]{4,3,2,1,0:T(2,128)} %param.21) | copy-start | bytes 1540
  119.8 18.2 %copy-start.18 = (pred[2,64]{1,0:T(4,128)(4,1)S(1)}, pred[2,64]{1,0:T(4,128)(4,1)}, u32[]{:S(2)}) copy-start(pred[2,64]{1,0:T(4,128)(4,1)} %copy-done.16) | copy-start | bytes 388
  133.6 21.9 %collective-permute-start.12 = (f32[6,1,16,128]{3,0,2,1:T(8,128)S(1)}, f32[6,1,16,128]{3,0,2,1:T(8,128)S(1)}, u32[]{:S(2)}, u32[]{:S(2)}) collective-permute-start(f32[6,1,16,128]{3,0,2,1:T(8,128)S(1)} %get-tuple-element.21), channel_id=1, source_target_pairs={{8,0},{16,8},{24,16},{9,1},{17,9},{25,17},{10,2},{18,10},{26,18},{... | collective-permute-start | bytes 147464 | tf_op jit(solution)/shard_map/ppermute | solution.py:17
  135.0 20.5 %collective-permute-start.13 = (f32[6,1,16,128]{3,0,2,1:T(8,128)S(1)}, f32[6,1,16,128]{3,0,2,1:T(8,128)S(1)}, u32[]{:S(2)}, u32[]{:S(2)}) collective-permute-start(f32[6,1,16,128]{3,0,2,1:T(8,128)S(1)} %get-tuple-element.20), channel_id=1, source_target_pairs={{0,8},{8,16},{16,24},{1,9},{9,17},{17,25},{2,10},{10,18},{18,26},{... | collective-permute-start | bytes 147464 | tf_op jit(solution)/shard_map/ppermute | solution.py:14
  145.4 17.5 %copy-start.4 = (f32[8,16,128]{2,1,0:T(8,128)S(1)}, f32[8,16,128]{2,1,0:T(8,128)}, u32[]{:S(2)}) copy-start(f32[8,16,128]{2,1,0:T(8,128)} %copy-done.2) | copy-start | bytes 196612
  155.5 9.7 %collective-permute-start.14 = (f32[6,10,1,128]{3,0,2,1:T(8,128)S(1)}, f32[6,10,1,128]{3,0,2,1:T(8,128)S(1)}, u32[]{:S(2)}, u32[]{:S(2)}) collective-permute-start(f32[6,10,1,128]{3,0,2,1:T(8,128)S(1)} %get-tuple-element.15), channel_id=1, source_target_pairs={{4,0},{5,1},{6,2},{7,3},{12,8},{13,9},{14,10},{15,11},{20,16},{21,... | collective-permute-start | bytes 92168 | tf_op jit(solution)/shard_map/ppermute | solution.py:17
  156.8 8.4 %collective-permute-start.15 = (f32[6,10,1,128]{3,0,2,1:T(8,128)S(1)}, f32[6,10,1,128]{3,0,2,1:T(8,128)S(1)}, u32[]{:S(2)}, u32[]{:S(2)}) collective-permute-start(f32[6,10,1,128]{3,0,2,1:T(8,128)S(1)} %get-tuple-element.14), channel_id=1, source_target_pairs={{0,4},{1,5},{2,6},{3,7},{8,12},{9,13},{10,14},{11,15},{16,20},{17,... | collective-permute-start | bytes 92168 | tf_op jit(solution)/shard_map/ppermute | solution.py:14
  165.2 0.6 copy-start.5
  167.3 15.4 %copy-start.10 = (f32[8,16,128]{2,1,0:T(8,128)S(1)}, f32[8,16,128]{2,1,0:T(8,128)}, u32[]{:S(2)}) copy-start(f32[8,16,128]{2,1,0:T(8,128)} %param.17) | copy-start | bytes 196612
  167.3 7.6 %collective-permute-start.17 = (f32[6,10,18,1]{2,3,1,0:T(1,128)}, f32[6,10,18,1]{2,3,1,0:T(1,128)S(1)}, u32[]{:S(2)}, u32[]{:S(2)}) collective-permute-start(f32[6,10,18,1]{2,3,1,0:T(1,128)} %copy.173), channel_id=1, source_target_pairs={{0,1},{1,2},{2,3},{4,5},{5,6},{6,7},{8,9},{9,10},{10,11},{12,13},{... | collective-permute-start | bytes 12968 | tf_op jit(solution)/shard_map/ppermute | solution.py:14
  171.4 5.8 %collective-permute-start.16 = (f32[6,10,18,1]{2,3,1,0:T(1,128)S(1)}, f32[6,10,18,1]{2,3,1,0:T(1,128)S(1)}, u32[]{:S(2)}, u32[]{:S(2)}) collective-permute-start(f32[6,10,18,1]{2,3,1,0:T(1,128)S(1)} %copy.170), channel_id=1, source_target_pairs={{1,0},{2,1},{3,2},{5,4},{6,5},{7,6},{9,8},{10,9},{11,10},{13,12},{... | collective-permute-start | bytes 12968 | tf_op jit(solution)/shard_map/ppermute | solution.py:17
where the time goes:
time: 185 us; the launch traced here: 183 us
  local copies, waits for them, and re-layouts  59 us (32%)
  starting transfers between devices  53.5 us (29%)
  matrix products  32.2 us (17%)
  other arithmetic  19.3 us (10%)
  blocking collectives  12.3 us (7%)
  waiting for transfers between devices  5.81 us (3%)
    ppermute x9, starting transfers between devices, with_halo(): lax.ppermute(lax.slice_in_dim(block, block.shape[dim] - width, None, axis...  34.1 us
    dot_general x18, matrix products, couple(): jnp.einsum('ji,jxyz->ixyz', block, field, precision=lax.Precision.HIGHEST)  30.8 us
    reshape x3, local copies, waits for them, and re-layouts, local(): coupled.at[:, received_targets].add(incoming.reshape(n_var, -1))  17.1 us
    reshape x3, local copies, waits for them, and re-layouts, local(): adjoint.reshape(n_var, -1)[:, source_index].reshape(n_var, n_span, slots)  15.9 us
    scatter-add x3, other arithmetic, local(): coupled.at[:, received_targets].add(incoming.reshape(n_var, -1))  14.6 us
    gather x3, local copies, waits for them, and re-layouts, local(): adjoint.reshape(n_var, -1)[:, source_index].reshape(n_var, n_span, slots)  12.3 us
    all_to_all x2, blocking collectives, local(): lax.all_to_all(outgoing, 'span', split_axis=1, concat_axis=1, tiled=True)  12.3 us
    ppermute x9, starting transfers between devices, with_halo(): lax.ppermute(lax.slice_in_dim(block, 0, width, axis=dim), axis, backward)  11.7 us
  transfers between devices with their start and end apart: 20, of which 4 were waited for; matrix products, arithmetic and copies ran while one was open for 39% of the time, Pallas kernels for 0%

commit v1 on v0

v1 whole, which is shorter than its diff:
```python
import functools

import jax
import jax.numpy as jnp
from jax import lax
from jax.experimental import pallas as pl
from jax.experimental.pallas import tpu as pltpu
from jax.sharding import PartitionSpec as P

SWEEPS = 3
LANES = 128
STEP = 2
MESH = pl.DeviceIdType.MESH
F32 = jnp.float32
BF16 = jnp.bfloat16


def iota(shape, dim):
    return lax.broadcasted_iota(jnp.int32, shape, dim)


def fiota(shape, dim):
    return iota(shape, dim).astype(F32)


def column(row, n):
    wide = jnp.broadcast_to(row.astype(F32), (n, n))
    return jnp.sum(jnp.where(iota((n, n), 0) == iota((n, n), 1), wide, 0.0), axis=1, keepdims=True)


def one_hots(cell):
    row = jnp.floor(cell * (1.0 / LANES))
    lane = fiota(cell.shape, 1)
    return jnp.where(row == lane, 1.0, 0.0), jnp.where(cell - row * LANES == lane, 1.0, 0.0)


def kernel(
    n_chord, n_span, n_wall, nv, cx, cy, slots,
    sens_hbm, diag_hbm, face_hbm, up_ref, low_ref, couple_ref, prod_hbm,
    send_ref, target_ref, orient_ref, weight_ref,
    out_ref, grad_ref,
    sens, rdiag, face, prod, adj, acc, halves,
    wall_out, wall_in, span_out, span_in, chord_in, span_term, wall_coef,
    iface_out, iface_in, cell_out, cell_in,
    pick_rows, pick_lanes, weights, put_rows, put_lanes, put_vals, put,
    load_sem, halo_send, halo_recv, iface_send, iface_recv, cell_send, cell_recv,
):
    total = n_span * slots
    chunks = cx // STEP
    ci, si, wi = lax.axis_index("chord"), lax.axis_index("span"), lax.axis_index("wall")
    places = (("chord", ci, n_chord), ("span", si, n_span), ("wall", wi, n_wall))

    def exists(axis, side):
        _, place, count = places[axis]
        return place > 0 if side == 0 else place < count - 1

    def neighbour(axis, side):
        name, place, _ = places[axis]
        return {name: place - 1 if side == 0 else place + 1}

    loads = [
        pltpu.make_async_copy(src, dst, load_sem.at[k])
        for k, (src, dst) in enumerate(
            ((sens_hbm, sens), (diag_hbm, rdiag), (face_hbm, face), (prod_hbm, prod))
        )
    ]
    for load in loads:
        load.start()

    barrier = pltpu.get_barrier_semaphore()
    for axis in (0, 2):
        for side in (0, 1):
            @pl.when(exists(axis, side))
            def _():
                pl.semaphore_signal(
                    barrier, inc=1, device_id=neighbour(axis, side), device_id_type=MESH
                )
    peers = [lax.rem(si + d, n_span) for d in range(1, n_span)]
    for peer in peers:
        pl.semaphore_signal(barrier, inc=1, device_id={"span": peer}, device_id_type=MESH)

    lane_id = iota((1, LANES), 1)
    for shift in range(-(nv - 1), nv):
        coef = jnp.zeros((1, LANES), F32)
        for i in range(nv):
            j = i + shift
            if 0 <= j < nv:
                mine = lane_id // (2 * cx) == i
                coef = jnp.where(mine & (lane_id % 2 == 0), up_ref[2, j, i], coef)
                coef = jnp.where(mine & (lane_id % 2 == 1), low_ref[2, j, i], coef)
        wall_coef[shift + nv - 1] = coef
    for buf in range(SWEEPS):
        for j in range(nv):
            adj[buf, j, 0] = jnp.zeros((cy, LANES), F32)
            adj[buf, j, cx + 1] = jnp.zeros((cy, LANES), F32)
    for sweep in range(SWEEPS):
        for side in (0, 1):
            @pl.when(jnp.logical_not(exists(0, side)))
            def _():
                chord_in[sweep, side] = jnp.zeros(chord_in.shape[2:], F32)

            @pl.when(jnp.logical_not(exists(1, side)))
            def _():
                span_in[sweep, side] = jnp.zeros(span_in.shape[2:], F32)

            @pl.when(jnp.logical_not(exists(2, side)))
            def _():
                wall_in[sweep, side] = jnp.zeros(wall_in.shape[2:], F32)

    table = []
    for o in range(2):
        rows = []
        for j in range(nv):
            row = jnp.zeros((1, LANES), F32)
            for i in range(nv):
                row = jnp.where(lane_id == i, couple_ref[o, j, i], row)
            rows.append(row)
        table.append(rows)
    send_all = send_ref[0, 0, 0]
    target_all = target_ref[0, 0, 0]
    orient_all = orient_ref[0, 0, 0]
    weight_all = weight_ref[0, 0, 0]
    for t in range(n_span):
        part = pl.ds(t * slots, slots)
        cell_out[t] = jnp.broadcast_to(column(target_all[t : t + 1], slots), (slots, LANES))
        cell = jnp.broadcast_to(column(send_all[t : t + 1], slots), (slots, LANES))
        rows, lanes = one_hots(cell)
        pick_rows[part, 0:LANES] = rows.astype(BF16)
        pick_rows[part, LANES : 2 * LANES] = rows.astype(BF16)
        pick_lanes[part] = lanes
        facing = column(orient_all[t : t + 1], slots)
        weight = column(weight_all[t : t + 1], slots)
        for j in range(nv):
            weights[j, part] = weight * jnp.where(facing == 1.0, table[1][j], table[0][j])

    greeted = n_span - 1
    for axis in (0, 2):
        for side in (0, 1):
            greeted = greeted + jnp.where(exists(axis, side), 1, 0)
    pl.semaphore_wait(barrier, greeted)

    def cell_copy(peer, slot):
        return pltpu.make_async_remote_copy(
            src_ref=cell_out.at[peer], dst_ref=cell_in.at[slot],
            send_sem=cell_send.at[peer], recv_sem=cell_recv.at[slot],
            device_id={"span": peer}, device_id_type=MESH,
        )

    for peer in peers:
        cell_copy(peer, si).start()
    cell_in[si] = cell_out[si]

    def halo_copy(sweep, axis, side):
        if axis == 0:
            src = adj.at[sweep, :, 1 if side == 0 else cx]
            dst = chord_in.at[sweep, 1 - side]
        elif axis == 1:
            src, dst = span_out.at[sweep, side], span_in.at[sweep, 1 - side]
        else:
            src, dst = wall_out.at[sweep], wall_in.at[sweep, 1 - side]
        return pltpu.make_async_remote_copy(
            src_ref=src, dst_ref=dst,
            send_sem=halo_send.at[sweep, 2 * axis + side],
            recv_sem=halo_recv.at[sweep, 2 * axis + 1 - side],
            device_id=neighbour(axis, side), device_id_type=MESH,
        )

    def each_halo(sweep, act):
        for axis in range(3):
            for side in (0, 1):
                @pl.when(exists(axis, side))
                def _():
                    act(axis, side)

    def start_halos(sweep):
        each_halo(sweep, lambda axis, side: halo_copy(sweep, axis, side).start())

    def wait_halos(sweep):
        each_halo(sweep, lambda axis, side: halo_copy(sweep, axis, 1 - side).wait_recv())

    def iface_copy(sweep, peer, slot):
        return pltpu.make_async_remote_copy(
            src_ref=iface_out.at[sweep, peer], dst_ref=iface_in.at[sweep, slot],
            send_sem=iface_send.at[sweep, peer], recv_sem=iface_recv.at[sweep, slot],
            device_id={"span": peer}, device_id_type=MESH,
        )

    lanes2d = iota((cy, LANES), 1)
    rows2d = iota((cy, LANES), 0)

    def keep(sweep, i, q, plane, value, packed):
        adj[sweep, i, plane + 1] = value
        high = value.astype(BF16)
        at = pl.multiple_of(plane * cy, cy)
        wide = pl.ds((i % 2) * LANES, LANES)
        halves[i // 2, pl.ds(at, cy), wide] = high
        halves[i // 2, pl.ds(cx * cy + at, cy), wide] = (value - high.astype(F32)).astype(BF16)
        span_out[sweep, 0, i, pl.ds(plane, 1)] = value[0:1]
        span_out[sweep, 1, i, pl.ds(plane, 1)] = value[cy - 1 : cy]
        pair = i * cx + plane
        turned = pltpu.roll(value, 2 * pair + 1, 1)
        return jnp.where(lanes2d // 2 == pair, turned, packed)

    loads[0].wait()
    loads[1].wait()

    def first(chunk, packed):
        for i in range(nv):
            for q in range(STEP):
                plane = chunk * STEP + q
                inverse = 1.0 / rdiag[i, plane]
                rdiag[i, plane] = inverse
                packed = keep(0, i, q, plane, sens[i, plane] * inverse, packed)
        return packed

    wall_out[0] = lax.fori_loop(0, chunks, first, jnp.zeros((cy, LANES), F32))
    start_halos(0)
    loads[2].wait()

    for sweep in range(SWEEPS):
        values = jnp.zeros((total, LANES), F32)
        for pair in range(nv // 2):
            picked = jnp.dot(pick_rows[...], halves[pair], preferred_element_type=F32)
            for h in range(2):
                own = picked[:, h * LANES : (h + 1) * LANES] * pick_lanes[...]
                values = values + jnp.sum(own, axis=1, keepdims=True) * weights[2 * pair + h]
        for t in range(n_span):
            iface_out[sweep, t] = values[t * slots : (t + 1) * slots]
        for peer in peers:
            iface_copy(sweep, peer, si).start()
        iface_in[sweep, si] = iface_out[sweep, si]

        def own_part(chunk, carry):
            at = chunk * STEP
            for axis in range(3):
                sums = [None] * nv
                for j in range(nv):
                    if axis == 0:
                        low = adj[sweep, j, pl.ds(at, STEP)].reshape(STEP * cy, LANES)
                        up = adj[sweep, j, pl.ds(at + 2, STEP)].reshape(STEP * cy, LANES)
                    else:
                        here = adj[sweep, j, pl.ds(at + 1, STEP)]
                        if axis == 1:
                            low = jnp.concatenate([pltpu.roll(here[q], 1, 0) for q in range(STEP)])
                            up = jnp.concatenate(
                                [pltpu.roll(here[q], cy - 1, 0) for q in range(STEP)]
                            )
                        else:
                            here = here.reshape(STEP * cy, LANES)
                            low = pltpu.roll(here, 1, 1)
                            up = pltpu.roll(here, LANES - 1, 1)
                    for i in range(nv):
                        term = up_ref[axis, j, i] * up + low_ref[axis, j, i] * low
                        sums[i] = term if j == 0 else sums[i] + term
                scale = face[axis, pl.ds(at, STEP)].reshape(STEP * cy, LANES)
                for i in range(nv):
                    base = sens if axis == 0 else acc
                    rest = base[i, pl.ds(at, STEP)].reshape(STEP * cy, LANES) - scale * sums[i]
                    acc[i, pl.ds(at, STEP)] = rest.reshape(STEP, cy, LANES)
            return carry

        lax.fori_loop(0, chunks, own_part, 0)

        wait_halos(sweep)

        for side in (0, 1):
            blocks = low_ref if side == 0 else up_ref
            edge = 0 if side == 0 else cx - 1
            for i in range(nv):
                chord_sum = None
                span_sum = None
                for j in range(nv):
                    chord_new = blocks[0, j, i] * chord_in[sweep, side, j]
                    span_new = blocks[1, j, i] * (span_in[sweep, side, j] - span_out[sweep, 1 - side, j])
                    chord_sum = chord_new if j == 0 else chord_sum + chord_new
                    span_sum = span_new if j == 0 else span_sum + span_new
                acc[i, edge] = acc[i, edge] - face[0, edge] * chord_sum
                span_term[side, i] = span_sum
        from_low = pltpu.roll(wall_in[sweep, 0] - wall_out[sweep], 1, 1)
        from_high = pltpu.roll(wall_in[sweep, 1] - wall_out[sweep], LANES - 1, 1)
        edges = jnp.where(lanes2d % 2 == 0, from_high, from_low)
        wall_term = jnp.zeros((cy, LANES), F32)
        for shift in range(-(nv - 1), nv):
            moved = edges if shift == 0 else pltpu.roll(edges, (-2 * cx * shift) % LANES, 1)
            wall_term = wall_term + wall_coef[shift + nv - 1] * moved

        if sweep == 0:
            for peer in peers:
                cell_copy(peer, peer).wait_recv()
            rows, lanes = one_hots(cell_in[...].reshape(total, LANES))
            put_lanes[...] = lanes
            turned = jnp.transpose(rows).astype(BF16)
            put_rows[:, 0:total] = turned
            put_rows[:, total : 2 * total] = turned
        for peer in peers:
            iface_copy(sweep, peer, peer).wait_recv()
        arrived = iface_in[sweep].reshape(total, LANES)
        for i in range(nv):
            spread = arrived[:, i : i + 1] * put_lanes[...]
            high = spread.astype(BF16)
            wide = slice((i % 2) * LANES, (i % 2 + 1) * LANES)
            put_vals[i // 2, 0:total, wide] = high
            put_vals[i // 2, total : 2 * total, wide] = (spread - high.astype(F32)).astype(BF16)
        for pair in range(nv // 2):
            put[pair] = jnp.dot(put_rows[...], put_vals[pair], preferred_element_type=F32)

        def finish(chunk, packed):
            for q in range(STEP):
                plane = chunk * STEP + q
                at = pl.multiple_of(plane * cy, cy)
                for i in range(nv):
                    turn = lax.rem(2 * LANES - 1 - 2 * (i * cx + plane), LANES)
                    wall = pltpu.roll(wall_term, turn, 1)
                    wall = jnp.where((lanes2d == 0) | (lanes2d == LANES - 1), wall, 0.0)
                    span = jnp.where(rows2d == 0, span_term[0, i, pl.ds(plane, 1)], 0.0)
                    span = jnp.where(rows2d == cy - 1, span_term[1, i, pl.ds(plane, 1)], span)
                    rest = acc[i, plane] - face[1, plane] * span - face[2, plane] * wall
                    rest = rest - put[i // 2, pl.ds(at, cy), pl.ds((i % 2) * LANES, LANES)]
                    value = rest * rdiag[i, plane]
                    if sweep < SWEEPS - 1:
                        packed = keep(sweep + 1, i, q, plane, value, packed)
                    else:
                        out_ref[i, plane] = value
                        if i == nv - 1:
                            grad_ref[plane] = prod[plane] * value
            return packed

        if sweep == SWEEPS - 1:
            loads[3].wait()
        packed = lax.fori_loop(0, chunks, finish, jnp.zeros((cy, LANES), F32))
        if sweep < SWEEPS - 1:
            wall_out[sweep + 1] = packed
            start_halos(sweep + 1)

    for peer in peers:
        cell_copy(peer, si).wait_send()
    for sweep in range(SWEEPS):
        each_halo(sweep, lambda axis, side: halo_copy(sweep, axis, side).wait_send())
        for peer in peers:
            iface_copy(sweep, peer, si).wait_send()


def solution(mesh):
    n_chord, n_span, n_wall = mesh.shape["chord"], mesh.shape["span"], mesh.shape["wall"]

    def local(
        sensitivity, diagonal, face_coef, upper_blocks, lower_blocks, iface_blocks, production,
        send_cell, target_cell, orient, iface_weight,
    ):
        nv, cx, cy, cz = sensitivity.shape
        slots = send_cell.shape[-1]
        total = n_span * slots
        pairs = nv // 2
        vmem = pl.BlockSpec(memory_space=pltpu.VMEM)
        smem = pl.BlockSpec(memory_space=pltpu.SMEM)
        hbm = pl.BlockSpec(memory_space=pl.ANY)
        dma = pltpu.SemaphoreType.DMA
        field = (nv, cx, cy, cz)
        return pl.pallas_call(
            functools.partial(kernel, n_chord, n_span, n_wall, nv, cx, cy, slots),
            out_shape=(
                jax.ShapeDtypeStruct(field, F32),
                jax.ShapeDtypeStruct((cx, cy, cz), F32),
            ),
            in_specs=[hbm, hbm, hbm, smem, smem, smem, hbm, vmem, vmem, vmem, vmem],
            out_specs=(vmem, vmem),
            scratch_shapes=[
                pltpu.VMEM(field, F32),
                pltpu.VMEM(field, F32),
                pltpu.VMEM((3, cx, cy, cz), F32),
                pltpu.VMEM((cx, cy, cz), F32),
                pltpu.VMEM((SWEEPS, nv, cx + 2, cy, cz), F32),
                pltpu.VMEM(field, F32),
                pltpu.VMEM((pairs, 2 * cx * cy, 2 * cz), BF16),
                pltpu.VMEM((SWEEPS, cy, LANES), F32),
                pltpu.VMEM((SWEEPS, 2, cy, LANES), F32),
                pltpu.VMEM((SWEEPS, 2, nv, cx, cz), F32),
                pltpu.VMEM((SWEEPS, 2, nv, cx, cz), F32),
                pltpu.VMEM((SWEEPS, 2, nv, cy, cz), F32),
                pltpu.VMEM((2, nv, cx, cz), F32),
                pltpu.VMEM((2 * nv - 1, 1, LANES), F32),
                pltpu.VMEM((SWEEPS, n_span, slots, LANES), F32),
                pltpu.VMEM((SWEEPS, n_span, slots, LANES), F32),
                pltpu.VMEM((n_span, slots, LANES), F32),
                pltpu.VMEM((n_span, slots, LANES), F32),
                pltpu.VMEM((total, 2 * LANES), BF16),
                pltpu.VMEM((total, LANES), F32),
                pltpu.VMEM((nv, total, LANES), F32),
                pltpu.VMEM((LANES, 2 * total), BF16),
                pltpu.VMEM((total, LANES), F32),
                pltpu.VMEM((pairs, 2 * total, 2 * LANES), BF16),
                pltpu.VMEM((pairs, LANES, 2 * LANES), F32),
                dma((4,)),
                dma((SWEEPS, 6)),
                dma((SWEEPS, 6)),
                dma((SWEEPS, n_span)),
                dma((SWEEPS, n_span)),
                dma((n_span,)),
                dma((n_span,)),
            ],
            compiler_params=pltpu.CompilerParams(
                collective_id=0, has_side_effects=True, vmem_limit_bytes=48 * 1024 * 1024
            ),
            cost_estimate=pl.CostEstimate(
                flops=2 * SWEEPS * 6 * nv * nv * cx * cy * cz,
                bytes_accessed=4 * (3 * nv + 5) * cx * cy * cz,
                transcendentals=0,
            ),
        )(
            sensitivity, diagonal, face_coef, upper_blocks, lower_blocks, iface_blocks, production,
            send_cell, target_cell, orient, iface_weight,
        )

    grid = P(None, "chord", "span", "wall")
    rows = P("chord", "span", "wall", None, None)
    return jax.shard_map(
        local,
        mesh=mesh,
        in_specs=(grid, grid, grid, P(), P(), P(), P("chord", "span", "wall"), rows, rows, rows, rows),
        out_specs=(grid, P("chord", "span", "wall")),
        check_vma=False,
    )
```

time: 185 us -> 28.9 us (0.16)
  starting transfers between devices: 53.5 us -> 0 us
  local copies, waits for them, and re-layouts: 59 us -> 7.92 us
  matrix products: 32.2 us -> 0 us
  Pallas kernels: 0 us -> 19.9 us
  other arithmetic: 19.3 us -> 0 us
  blocking collectives: 12.3 us -> 0 us
  waiting for transfers between devices: 5.81 us -> 0 us
    ppermute x18 -> x0, starting transfers between devices: 45.8 us -> none  [the longest x9 34.1 us: with_halo(): lax.ppermute(lax.slice_in_dim(block, block.shape[dim] - width, None, axis...]
    reshape x14 -> x0, local copies, waits for them, and re-layouts: 33.8 us -> none  [the longest x3 17.1 us: local(): coupled.at[:, received_targets].add(incoming.reshape(n_var, -1))]
    dot_general x24 -> x0, matrix products: 32.2 us -> none  [the longest x18 30.8 us: couple(): jnp.einsum('ji,jxyz->ixyz', block, field, precision=lax.Precision.HIGHEST)]
    pallas_call x0 -> x1, Pallas kernels: none -> 19.9 us  [local(): pl.pallas_call(functools.partial(kernel, n_chord, n_span, n_wall, nv, cx,...]
    scatter-add x3 -> x0, other arithmetic: 14.6 us -> none  [local(): coupled.at[:, received_targets].add(incoming.reshape(n_var, -1))]
    gather x3 -> x0, local copies, waits for them, and re-layouts: 12.3 us -> none  [local(): adjoint.reshape(n_var, -1)[:, source_index].reshape(n_var, n_span, slots)]
    all_to_all x2 -> x0, blocking collectives: 12.3 us -> none  [local(): lax.all_to_all(outgoing, 'span', split_axis=1, concat_axis=1, tiled=True)]
    all_to_all x2 -> x0, starting transfers between devices: 7.64 us -> none  [the longest x1 4.35 us: local(): lax.all_to_all(target_cell.reshape(n_span, slots), 'span', split_axis=0,...]
  transfers between devices with their start and end apart: 20 -> 0, of which waited for: 4 -> 0; matrix products, arithmetic and copies ran while one was open for 39% -> 0% of each run, Pallas kernels for 0% -> 0%
where the time goes in v1:
time: 28.9 us; the launch traced here: 28.5 us
  Pallas kernels  19.9 us (69%)
  local copies, waits for them, and re-layouts  7.92 us (27%)
  between operations  0.68 us (2%)
    pallas_call x1, Pallas kernels, local(): pl.pallas_call(functools.partial(kernel, n_chord, n_span, n_wall, nv, cx,...  19.9 us
    unnamed x23, local copies, waits for them, and re-layouts  7.92 us

profile of v1, /device:TPU:0, one launch (start us, length us, event | category | flops | bytes accessed | tf_op | source)
XLA Modules:
  0.0 28.5 jit_solution(15328809355932705557)
XLA Ops:
  0.6 0.0 copy-start.7
  0.6 0.0 copy-start.6
  0.7 0.0 copy-start.4
  0.7 0.7 %copy.13.couple_ref = f32[2,6,6]{2,1,0:T(8,128)S(1)} copy(f32[2,6,6]{2,0,1:T(2,128)} %param.16) | data formatting | bytes 576 | tf_op args[5]
  1.4 0.0 copy-done.7
  1.4 0.0 copy-done.6
  1.4 0.0 copy-done.4
  1.4 0.0 copy-start
  1.4 1.0 %copy-done = f32[6,8,16,128]{3,2,1,0:T(8,128)S(1)} copy-done((f32[6,8,16,128]{3,2,1,0:T(8,128)S(1)}, f32[6,8,16,128]{3,2,1,0:T(8,128)}, u32[]{:S(2)}) %copy-start) | copy-done | bytes 393240
  2.4 0.0 copy-start.1
  2.4 1.0 %copy-done.1 = f32[6,8,16,128]{3,2,1,0:T(8,128)S(1)} copy-done((f32[6,8,16,128]{3,2,1,0:T(8,128)S(1)}, f32[6,8,16,128]{3,2,1,0:T(8,128)}, u32[]{:S(2)}) %copy-start.1) | copy-done | bytes 393240
  3.4 0.0 copy-start.2
  3.4 0.9 %copy-done.2 = f32[3,8,16,128]{3,2,1,0:T(8,128)S(1)} copy-done((f32[3,8,16,128]{3,2,1,0:T(8,128)S(1)}, f32[3,8,16,128]{3,2,1,0:T(8,128)}, u32[]{:S(2)}) %copy-start.2) | copy-done | bytes 196632
  4.3 0.0 copy-start.3
  4.3 0.8 %copy-done.3 = f32[8,16,128]{2,1,0:T(8,128)S(1)} copy-done((f32[8,16,128]{2,1,0:T(8,128)S(1)}, f32[8,16,128]{2,1,0:T(8,128)}, u32[]{:S(2)}) %copy-start.3) | copy-done | bytes 65560
  5.1 0.0 copy-start.5
  5.1 0.7 %copy-done.5 = f32[3,6,6]{2,1,0:T(8,128)S(1)} copy-done((f32[3,6,6]{2,1,0:T(8,128)S(1)}, f32[3,6,6]{2,1,0:T(8,128)}, u32[]{:S(2)}) %copy-start.5) | copy-done | bytes 456
  5.9 0.0 copy-start.8
  5.9 0.7 %copy-done.8 = s32[1,1,1,2,64]{4,3,2,1,0:T(2,128)S(1)} copy-done((s32[1,1,1,2,64]{4,3,2,1,0:T(2,128)S(1)}, s32[1,1,1,2,64]{4,3,2,1,0:T(2,128)}, u32[]{:S(2)}) %copy-start.8) | copy-done | bytes 536
  6.5 0.0 copy-start.9
  6.5 0.7 %copy-done.9 = f32[1,1,1,2,64]{4,3,2,1,0:T(2,128)S(1)} copy-done((f32[1,1,1,2,64]{4,3,2,1,0:T(2,128)S(1)}, f32[1,1,1,2,64]{4,3,2,1,0:T(2,128)}, u32[]{:S(2)}) %copy-start.9) | copy-done | bytes 536
  7.2 19.9 %shard_map.122 = (f32[6,8,16,128]{3,2,1,0:T(8,128)S(1)}, f32[8,16,128]{2,1,0:T(8,128)S(1)}) custom-call(f32[6,8,16,128]{3,2,1,0:T(8,128)S(1)} %copy-done, f32[6,8,16,128]{3,2,1,0:T(8,128)S(1)} %copy-done.1, f32[3,8,16,128]{3,2,1,0:T(8,128)S(1)} %copy-done.2, f32[3,6,6]{2,1,0:T(8,128)S(1)} %copy-done.4, f32[3,6,6]{2,1,0:T(8,128)S(1)} %copy-done.5, ...), custom_call_target="tpu_custom_call" | custom-call | flops 21233664 | bytes 1507328 | tf_op jit(solution)/shard_map/pallas_call | solution.py:359
  27.1 0.7 %copy.16 = f32[6,8,16,128]{3,2,1,0:T(8,128)} copy(f32[6,8,16,128]{3,2,1,0:T(8,128)S(1)} %get-tuple-element.4) | data formatting | bytes 786432
  27.8 0.6 %copy.17 = f32[8,16,128]{2,1,0:T(8,128)} copy(f32[8,16,128]{2,1,0:T(8,128)S(1)} %get-tuple-element.5) | data formatting | bytes 131072
Async XLA Ops:
  0.6 0.7 %copy-start.7 = (s32[1,1,1,2,64]{4,3,2,1,0:T(2,128)S(1)}, s32[1,1,1,2,64]{4,3,2,1,0:T(2,128)}, u32[]{:S(2)}) copy-start(s32[1,1,1,2,64]{4,3,2,1,0:T(2,128)} %target_ref.1) | copy-start | bytes 1540
  0.6 0.7 %copy-start.6 = (s32[1,1,1,2,64]{4,3,2,1,0:T(2,128)S(1)}, s32[1,1,1,2,64]{4,3,2,1,0:T(2,128)}, u32[]{:S(2)}) copy-start(s32[1,1,1,2,64]{4,3,2,1,0:T(2,128)} %send_ref.1) | copy-start | bytes 1540
  0.7 0.7 %copy-start.4 = (f32[3,6,6]{2,1,0:T(8,128)S(1)}, f32[3,6,6]{2,1,0:T(8,128)}, u32[]{:S(2)}) copy-start(f32[3,6,6]{2,1,0:T(8,128)} %up_ref.1) | copy-start | bytes 1300
  1.4 1.0 %copy-start = (f32[6,8,16,128]{3,2,1,0:T(8,128)S(1)}, f32[6,8,16,128]{3,2,1,0:T(8,128)}, u32[]{:S(2)}) copy-start(f32[6,8,16,128]{3,2,1,0:T(8,128)} %sens_hbm.1) | copy-start | bytes 1179652
  2.4 1.0 %copy-start.1 = (f32[6,8,16,128]{3,2,1,0:T(8,128)S(1)}, f32[6,8,16,128]{3,2,1,0:T(8,128)}, u32[]{:S(2)}) copy-start(f32[6,8,16,128]{3,2,1,0:T(8,128)} %diag_hbm.1) | copy-start | bytes 1179652
  3.4 0.9 %copy-start.2 = (f32[3,8,16,128]{3,2,1,0:T(8,128)S(1)}, f32[3,8,16,128]{3,2,1,0:T(8,128)}, u32[]{:S(2)}) copy-start(f32[3,8,16,128]{3,2,1,0:T(8,128)} %face_hbm.1) | copy-start | bytes 589828
  4.3 0.8 %copy-start.3 = (f32[8,16,128]{2,1,0:T(8,128)S(1)}, f32[8,16,128]{2,1,0:T(8,128)}, u32[]{:S(2)}) copy-start(f32[8,16,128]{2,1,0:T(8,128)} %prod_hbm.1) | copy-start | bytes 196612
  5.1 0.7 %copy-start.5 = (f32[3,6,6]{2,1,0:T(8,128)S(1)}, f32[3,6,6]{2,1,0:T(8,128)}, u32[]{:S(2)}) copy-start(f32[3,6,6]{2,1,0:T(8,128)} %low_ref.1) | copy-start | bytes 1300
  5.9 0.7 %copy-start.8 = (s32[1,1,1,2,64]{4,3,2,1,0:T(2,128)S(1)}, s32[1,1,1,2,64]{4,3,2,1,0:T(2,128)}, u32[]{:S(2)}) copy-start(s32[1,1,1,2,64]{4,3,2,1,0:T(2,128)} %orient_ref.1) | copy-start | bytes 1540
  6.5 0.7 %copy-start.9 = (f32[1,1,1,2,64]{4,3,2,1,0:T(2,128)S(1)}, f32[1,1,1,2,64]{4,3,2,1,0:T(2,128)}, u32[]{:S(2)}) copy-start(f32[1,1,1,2,64]{4,3,2,1,0:T(2,128)} %weight_ref.1) | copy-start | bytes 1540

commit v2 on v1

--- a/solution.py
+++ b/solution.py
@@ -36,14 +36,15 @@
 
 def kernel(
     n_chord, n_span, n_wall, nv, cx, cy, slots,
-    sens_hbm, diag_hbm, face_hbm, up_ref, low_ref, couple_ref, prod_hbm,
-    send_ref, target_ref, orient_ref, weight_ref,
-    out_ref, grad_ref,
-    sens, rdiag, face, prod, adj, acc, halves,
+    sens_hbm, diag_hbm, face_hbm, up_hbm, low_hbm, couple_hbm,
+    send_hbm, target_hbm, orient_hbm, weight_hbm,
+    out_hbm,
+    up_ref, low_ref, couple_ref, send_ref, target_ref, orient_ref, weight_ref,
+    sens, rdiag, face, adj, acc, halves,
     wall_out, wall_in, span_out, span_in, chord_in, span_term, wall_coef,
     iface_out, iface_in, cell_out, cell_in,
     pick_rows, pick_lanes, weights, put_rows, put_lanes, put_vals, put,
-    load_sem, halo_send, halo_recv, iface_send, iface_recv, cell_send, cell_recv,
+    load_sem, store_sem, halo_send, halo_recv, iface_send, iface_recv, cell_send, cell_recv,
 ):
     total = n_span * slots
     chunks = cx // STEP
@@ -61,7 +62,12 @@
     loads = [
         pltpu.make_async_copy(src, dst, load_sem.at[k])
         for k, (src, dst) in enumerate(
-            ((sens_hbm, sens), (diag_hbm, rdiag), (face_hbm, face), (prod_hbm, prod))
+            (
+                (sens_hbm, sens), (diag_hbm, rdiag), (face_hbm, face),
+                (up_hbm, up_ref), (low_hbm, low_ref), (couple_hbm, couple_ref),
+                (send_hbm, send_ref), (target_hbm, target_ref),
+                (orient_hbm, orient_ref), (weight_hbm, weight_ref),
+            )
         )
     ]
     for load in loads:
@@ -79,6 +85,109 @@
     for peer in peers:
         pl.semaphore_signal(barrier, inc=1, device_id={"span": peer}, device_id_type=MESH)
 
+    for buf in range(SWEEPS):
+        for j in range(nv):
+            adj[buf, j, 0] = jnp.zeros((cy, LANES), F32)
+            adj[buf, j, cx + 1] = jnp.zeros((cy, LANES), F32)
+    for sweep in range(SWEEPS):
+        for side in (0, 1):
+            @pl.when(jnp.logical_not(exists(0, side)))
+            def _():
+                chord_in[sweep, side] = jnp.zeros(chord_in.shape[2:], F32)
+
+            @pl.when(jnp.logical_not(exists(1, side)))
+            def _():
+                span_in[sweep, side] = jnp.zeros(span_in.shape[2:], F32)
+
+            @pl.when(jnp.logical_not(exists(2, side)))
+            def _():
+                wall_in[sweep, side] = jnp.zeros(wall_in.shape[2:], F32)
+
+    def cell_copy(peer, slot):
+        return pltpu.make_async_remote_copy(
+            src_ref=cell_out.at[peer], dst_ref=cell_in.at[slot],
+            send_sem=cell_send.at[peer], recv_sem=cell_recv.at[slot],
+            device_id={"span": peer}, device_id_type=MESH,
+        )
+
+    def halo_copy(sweep, axis, side):
+        if axis == 0:
+            src = adj.at[sweep, :, 1 if side == 0 else cx]
+            dst = chord_in.at[sweep, 1 - side]
+        elif axis == 1:
+            src, dst = span_out.at[sweep, side], span_in.at[sweep, 1 - side]
+        else:
+            src, dst = wall_out.at[sweep], wall_in.at[sweep, 1 - side]
+        return pltpu.make_async_remote_copy(
+            src_ref=src, dst_ref=dst,
+            send_sem=halo_send.at[sweep, 2 * axis + side],
+            recv_sem=halo_recv.at[sweep, 2 * axis + 1 - side],
+            device_id=neighbour(axis, side), device_id_type=MESH,
+        )
+
+    def each_halo(sweep, act):
+        for axis in range(3):
+            for side in (0, 1):
+                @pl.when(exists(axis, side))
+                def _():
+                    act(axis, side)
+
+    def start_halos(sweep):
+        each_halo(sweep, lambda axis, side: halo_copy(sweep, axis, side).start())
+
+    def wait_halos(sweep):
+        each_halo(sweep, lambda axis, side: halo_copy(sweep, axis, 1 - side).wait_recv())
+
+    def iface_copy(sweep, peer, slot):
+        return pltpu.make_async_remote_copy(
+            src_ref=iface_out.at[sweep, peer], dst_ref=iface_in.at[sweep, slot],
+            send_sem=iface_send.at[sweep, peer], recv_sem=iface_recv.at[sweep, slot],
+            device_id={"span": peer}, device_id_type=MESH,
+        )
+
+    lanes2d = iota((cy, LANES), 1)
+    rows2d = iota((cy, LANES), 0)
+
+    def keep(sweep, i, q, plane, value, packed):
+        adj[sweep, i, plane + 1] = value
+        high = value.astype(BF16)
+        at = pl.multiple_of(plane * cy, cy)
+        wide = pl.ds((i % 2) * LANES, LANES)
+        halves[i // 2, pl.ds(at, cy), wide] = high
+        halves[i // 2, pl.ds(cx * cy + at, cy), wide] = (value - high.astype(F32)).astype(BF16)
+        span_out[sweep, 0, i, pl.ds(plane, 1)] = value[0:1]
+        span_out[sweep, 1, i, pl.ds(plane, 1)] = value[cy - 1 : cy]
+        pair = i * cx + plane
+        turned = pltpu.roll(value, 2 * pair + 1, 1)
+        return jnp.where(lanes2d // 2 == pair, turned, packed)
+
+    def store(chunk):
+        planes = pl.ds(chunk * STEP, STEP)
+        return pltpu.make_async_copy(
+            acc.at[:, planes], out_hbm.at[:, planes], store_sem.at[chunk]
+        )
+
+    loads[0].wait()
+    loads[1].wait()
+
+    def first(chunk, packed):
+        for i in range(nv):
+            for q in range(STEP):
+                plane = chunk * STEP + q
+                inverse = 1.0 / rdiag[i, plane]
+                rdiag[i, plane] = inverse
+                packed = keep(0, i, q, plane, sens[i, plane] * inverse, packed)
+        return packed
+
+    wall_out[0] = lax.fori_loop(0, chunks, first, jnp.zeros((cy, LANES), F32))
+    greeted = n_span - 1
+    for axis in (0, 2):
+        for side in (0, 1):
+            greeted = greeted + jnp.where(exists(axis, side), 1, 0)
+    pl.semaphore_wait(barrier, greeted)
+    start_halos(0)
+    for k in range(3, 10):
+        loads[k].wait()
     lane_id = iota((1, LANES), 1)
     for shift in range(-(nv - 1), nv):
         coef = jnp.zeros((1, LANES), F32)
@@ -89,31 +198,13 @@
                 coef = jnp.where(mine & (lane_id % 2 == 0), up_ref[2, j, i], coef)
                 coef = jnp.where(mine & (lane_id % 2 == 1), low_ref[2, j, i], coef)
         wall_coef[shift + nv - 1] = coef
-    for buf in range(SWEEPS):
-        for j in range(nv):
-            adj[buf, j, 0] = jnp.zeros((cy, LANES), F32)
-            adj[buf, j, cx + 1] = jnp.zeros((cy, LANES), F32)
-    for sweep in range(SWEEPS):
-        for side in (0, 1):
-            @pl.when(jnp.logical_not(exists(0, side)))
-            def _():
-                chord_in[sweep, side] = jnp.zeros(chord_in.shape[2:], F32)
-
-            @pl.when(jnp.logical_not(exists(1, side)))
-            def _():
-                span_in[sweep, side] = jnp.zeros(span_in.shape[2:], F32)
-
-            @pl.when(jnp.logical_not(exists(2, side)))
-            def _():
-                wall_in[sweep, side] = jnp.zeros(wall_in.shape[2:], F32)
-
     table = []
     for o in range(2):
         rows = []
         for j in range(nv):
             row = jnp.zeros((1, LANES), F32)
             for i in range(nv):
-                row = jnp.where(lane_id == i, couple_ref[o, j, i], row)
+                row = jnp.where(lane_id == i, couple_ref[j, o, i], row)
             rows.append(row)
         table.append(rows)
     send_all = send_ref[0, 0, 0]
@@ -133,88 +224,9 @@
         for j in range(nv):
             weights[j, part] = weight * jnp.where(facing == 1.0, table[1][j], table[0][j])
 
-    greeted = n_span - 1
-    for axis in (0, 2):
-        for side in (0, 1):
-            greeted = greeted + jnp.where(exists(axis, side), 1, 0)
-    pl.semaphore_wait(barrier, greeted)
-
-    def cell_copy(peer, slot):
-        return pltpu.make_async_remote_copy(
-            src_ref=cell_out.at[peer], dst_ref=cell_in.at[slot],
-            send_sem=cell_send.at[peer], recv_sem=cell_recv.at[slot],
-            device_id={"span": peer}, device_id_type=MESH,
-        )
-
     for peer in peers:
         cell_copy(peer, si).start()
     cell_in[si] = cell_out[si]
-
-    def halo_copy(sweep, axis, side):
-        if axis == 0:
-            src = adj.at[sweep, :, 1 if side == 0 else cx]
-            dst = chord_in.at[sweep, 1 - side]
-        elif axis == 1:
-            src, dst = span_out.at[sweep, side], span_in.at[sweep, 1 - side]
-        else:
-            src, dst = wall_out.at[sweep], wall_in.at[sweep, 1 - side]
-        return pltpu.make_async_remote_copy(
-            src_ref=src, dst_ref=dst,
-            send_sem=halo_send.at[sweep, 2 * axis + side],
-            recv_sem=halo_recv.at[sweep, 2 * axis + 1 - side],
-            device_id=neighbour(axis, side), device_id_type=MESH,
-        )
-
-    def each_halo(sweep, act):
-        for axis in range(3):
-            for side in (0, 1):
-                @pl.when(exists(axis, side))
-                def _():
-                    act(axis, side)
-
-    def start_halos(sweep):
-        each_halo(sweep, lambda axis, side: halo_copy(sweep, axis, side).start())
-
-    def wait_halos(sweep):
-        each_halo(sweep, lambda axis, side: halo_copy(sweep, axis, 1 - side).wait_recv())
-
-    def iface_copy(sweep, peer, slot):
-        return pltpu.make_async_remote_copy(
-            src_ref=iface_out.at[sweep, peer], dst_ref=iface_in.at[sweep, slot],
-            send_sem=iface_send.at[sweep, peer], recv_sem=iface_recv.at[sweep, slot],
-            device_id={"span": peer}, device_id_type=MESH,
-        )
-
-    lanes2d = iota((cy, LANES), 1)
-    rows2d = iota((cy, LANES), 0)
-
-    def keep(sweep, i, q, plane, value, packed):
-        adj[sweep, i, plane + 1] = value
-        high = value.astype(BF16)
-        at = pl.multiple_of(plane * cy, cy)
-        wide = pl.ds((i % 2) * LANES, LANES)
-        halves[i // 2, pl.ds(at, cy), wide] = high
-        halves[i // 2, pl.ds(cx * cy + at, cy), wide] = (value - high.astype(F32)).astype(BF16)
-        span_out[sweep, 0, i, pl.ds(plane, 1)] = value[0:1]
-        span_out[sweep, 1, i, pl.ds(plane, 1)] = value[cy - 1 : cy]
-        pair = i * cx + plane
-        turned = pltpu.roll(value, 2 * pair + 1, 1)
-        return jnp.where(lanes2d // 2 == pair, turned, packed)
-
-    loads[0].wait()
-    loads[1].wait()
-
-    def first(chunk, packed):
-        for i in range(nv):
-            for q in range(STEP):
-                plane = chunk * STEP + q
-                inverse = 1.0 / rdiag[i, plane]
-                rdiag[i, plane] = inverse
-                packed = keep(0, i, q, plane, sens[i, plane] * inverse, packed)
-        return packed
-
-    wall_out[0] = lax.fori_loop(0, chunks, first, jnp.zeros((cy, LANES), F32))
-    start_halos(0)
     loads[2].wait()
 
     for sweep in range(SWEEPS):
@@ -320,18 +332,18 @@
                     if sweep < SWEEPS - 1:
                         packed = keep(sweep + 1, i, q, plane, value, packed)
                     else:
-                        out_ref[i, plane] = value
-                        if i == nv - 1:
-                            grad_ref[plane] = prod[plane] * value
+                        acc[i, plane] = value
+            if sweep == SWEEPS - 1:
+                store(chunk).start()
             return packed
 
-        if sweep == SWEEPS - 1:
-            loads[3].wait()
         packed = lax.fori_loop(0, chunks, finish, jnp.zeros((cy, LANES), F32))
         if sweep < SWEEPS - 1:
             wall_out[sweep + 1] = packed
             start_halos(sweep + 1)
 
+    for chunk in range(chunks):
+        store(chunk).wait()
     for peer in peers:
         cell_copy(peer, si).wait_send()
     for sweep in range(SWEEPS):
@@ -351,24 +363,25 @@
         slots = send_cell.shape[-1]
         total = n_span * slots
         pairs = nv // 2
-        vmem = pl.BlockSpec(memory_space=pltpu.VMEM)
-        smem = pl.BlockSpec(memory_space=pltpu.SMEM)
-        hbm = pl.BlockSpec(memory_space=pl.ANY)
+        hbm = pl.BlockSpec(memory_space=pltpu.HBM)
         dma = pltpu.SemaphoreType.DMA
         field = (nv, cx, cy, cz)
-        return pl.pallas_call(
+        adjoint = pl.pallas_call(
             functools.partial(kernel, n_chord, n_span, n_wall, nv, cx, cy, slots),
-            out_shape=(
-                jax.ShapeDtypeStruct(field, F32),
-                jax.ShapeDtypeStruct((cx, cy, cz), F32),
-            ),
-            in_specs=[hbm, hbm, hbm, smem, smem, smem, hbm, vmem, vmem, vmem, vmem],
-            out_specs=(vmem, vmem),
+            out_shape=jax.ShapeDtypeStruct(field, F32),
+            in_specs=[hbm] * 10,
+            out_specs=hbm,
             scratch_shapes=[
+                pltpu.SMEM(upper_blocks.shape, F32),
+                pltpu.SMEM(lower_blocks.shape, F32),
+                pltpu.SMEM((nv, 2, nv), F32),
+                pltpu.VMEM(send_cell.shape, jnp.int32),
+                pltpu.VMEM(target_cell.shape, jnp.int32),
+                pltpu.VMEM(orient.shape, jnp.int32),
+                pltpu.VMEM(iface_weight.shape, F32),
                 pltpu.VMEM(field, F32),
                 pltpu.VMEM(field, F32),
                 pltpu.VMEM((3, cx, cy, cz), F32),
-                pltpu.VMEM((cx, cy, cz), F32),
                 pltpu.VMEM((SWEEPS, nv, cx + 2, cy, cz), F32),
                 pltpu.VMEM(field, F32),
                 pltpu.VMEM((pairs, 2 * cx * cy, 2 * cz), BF16),
@@ -390,7 +403,8 @@
                 pltpu.VMEM((total, LANES), F32),
                 pltpu.VMEM((pairs, 2 * total, 2 * LANES), BF16),
                 pltpu.VMEM((pairs, LANES, 2 * LANES), F32),
-                dma((4,)),
+                dma((10,)),
+                dma((cx // STEP,)),
                 dma((SWEEPS, 6)),
                 dma((SWEEPS, 6)),
                 dma((SWEEPS, n_span)),
@@ -399,7 +413,7 @@
                 dma((n_span,)),
             ],
             compiler_params=pltpu.CompilerParams(
-                collective_id=0, has_side_effects=True, vmem_limit_bytes=48 * 1024 * 1024
+                collective_id=0, has_side_effects=True, vmem_limit_bytes=125 * 512 * 1024
             ),
             cost_estimate=pl.CostEstimate(
                 flops=2 * SWEEPS * 6 * nv * nv * cx * cy * cz,
@@ -407,9 +421,10 @@
                 transcendentals=0,
             ),
         )(
-            sensitivity, diagonal, face_coef, upper_blocks, lower_blocks, iface_blocks, production,
-            send_cell, target_cell, orient, iface_weight,
-        )
+            sensitivity, diagonal, face_coef, upper_blocks, lower_blocks,
+            iface_blocks.transpose(1, 0, 2), send_cell, target_cell, orient, iface_weight,
+        )
+        return adjoint, production * adjoint[nv - 1]
 
     grid = P(None, "chord", "span", "wall")
     rows = P("chord", "span", "wall", None, None)

time: 28.9 us -> 22.9 us (0.79)
  local copies, waits for them, and re-layouts: 7.92 us -> 1.78 us
  other arithmetic: 0 us -> 1.48 us
  Pallas kernels: 19.9 us -> 18.7 us
    unnamed x23 -> x3, local copies, waits for them, and re-layouts: 7.92 us -> 1.78 us
    mul x0 -> x1, other arithmetic: none -> 1.48 us  [local(): return (adjoint, production * adjoint[nv - 1])]
    pallas_call x1, Pallas kernels: 19.9 us -> 18.7 us  [local(): pl.pallas_call(functools.partial(kernel, n_chord, n_span, n_wall, nv, cx,...]
where the time goes in v2:
time: 22.9 us; the launch traced here: 22.7 us
  Pallas kernels  18.7 us (82%)
  local copies, waits for them, and re-layouts  1.78 us (8%)
  other arithmetic  1.48 us (6%)
  between operations  0.66 us (3%)
    pallas_call x1, Pallas kernels, local(): pl.pallas_call(functools.partial(kernel, n_chord, n_span, n_wall, nv, cx,...  18.7 us
    unnamed x3, local copies, waits for them, and re-layouts  1.78 us
    mul x1, other arithmetic, local(): return (adjoint, production * adjoint[nv - 1])  1.48 us

profile of v2, /device:TPU:0, one launch (start us, length us, event | category | flops | bytes accessed | tf_op | source)
XLA Modules:
  0.0 22.7 jit_solution(10638539225533319097)
XLA Ops:
  0.6 0.0 copy-start
  0.6 18.7 %shard_map.122 = f32[6,8,16,128]{3,2,1,0:T(8,128)} custom-call(f32[6,8,16,128]{3,2,1,0:T(8,128)} %sens_hbm.1, f32[6,8,16,128]{3,2,1,0:T(8,128)} %diag_hbm.1, f32[3,8,16,128]{3,2,1,0:T(8,128)} %face_hbm.1, f32[3,6,6]{2,1,0:T(8,128)} %up_hbm.1, f32[3,6,6]{2,1,0:T(8,128)} %low_hbm.1, f32[6,2,6]{2,1,0:T(2,128)} %bitcast.3, s32[1,1,1,2,64]{4,3,2,1,0:T(2,128)} %send_hbm.1, ...), custom_call_target="tpu_custom_call" | custom-call | flops 21233664 | bytes 1507328 | tf_op jit(solution)/shard_map/pallas_call | solution.py:369
  19.4 0.0 copy-done
  19.4 1.5 %bitcast_multiply_fusion = f32[8,16,128]{2,1,0:T(8,128)} fusion(f32[8,16,128]{2,1,0:T(8,128)S(1)} %copy-done, f32[6,8,16,128]{3,2,1,0:T(8,128)} %shard_map.122), kind=kLoop, calls=%fused_computation | loop fusion | flops 16384 | bytes 196608 | tf_op jit(solution)/shard_map/mul | solution.py:427
  20.9 1.8 %copy.14 = f32[6,8,16,128]{3,2,1,0:T(8,128)} copy(f32[6,8,16,128]{3,2,1,0:T(8,128)} %shard_map.122) | data formatting | bytes 786432
Async XLA Ops:
  0.6 18.8 %copy-start = (f32[8,16,128]{2,1,0:T(8,128)S(1)}, f32[8,16,128]{2,1,0:T(8,128)}, u32[]{:S(2)}) copy-start(f32[8,16,128]{2,1,0:T(8,128)} %param.17) | copy-start | bytes 196612

commit v3 on v2

--- a/solution.py
+++ b/solution.py
@@ -36,15 +36,15 @@
 
 def kernel(
     n_chord, n_span, n_wall, nv, cx, cy, slots,
-    sens_hbm, diag_hbm, face_hbm, up_hbm, low_hbm, couple_hbm,
+    sens_hbm, diag_hbm, face_hbm, up_hbm, low_hbm, couple_hbm, prod_hbm,
     send_hbm, target_hbm, orient_hbm, weight_hbm,
-    out_hbm,
+    out_hbm, grad_hbm,
     up_ref, low_ref, couple_ref, send_ref, target_ref, orient_ref, weight_ref,
-    sens, rdiag, face, adj, acc, halves,
+    sens, rdiag, face, prod, adj, acc, halves,
     wall_out, wall_in, span_out, span_in, chord_in, span_term, wall_coef,
     iface_out, iface_in, cell_out, cell_in,
     pick_rows, pick_lanes, weights, put_rows, put_lanes, put_vals, put,
-    load_sem, store_sem, halo_send, halo_recv, iface_send, iface_recv, cell_send, cell_recv,
+    load_sem, store_sem, grad_sem, halo_send, halo_recv, iface_send, iface_recv, cell_send, cell_recv,
 ):
     total = n_span * slots
     chunks = cx // STEP
@@ -67,6 +67,7 @@
                 (up_hbm, up_ref), (low_hbm, low_ref), (couple_hbm, couple_ref),
                 (send_hbm, send_ref), (target_hbm, target_ref),
                 (orient_hbm, orient_ref), (weight_hbm, weight_ref),
+                (prod_hbm, prod),
             )
         )
     ]
@@ -163,8 +164,9 @@
 
     def store(chunk):
         planes = pl.ds(chunk * STEP, STEP)
-        return pltpu.make_async_copy(
-            acc.at[:, planes], out_hbm.at[:, planes], store_sem.at[chunk]
+        return (
+            pltpu.make_async_copy(prod.at[planes], grad_hbm.at[planes], grad_sem.at[chunk]),
+            pltpu.make_async_copy(acc.at[:, planes], out_hbm.at[:, planes], store_sem.at[chunk]),
         )
 
     loads[0].wait()
@@ -333,17 +335,23 @@
                         packed = keep(sweep + 1, i, q, plane, value, packed)
                     else:
                         acc[i, plane] = value
+                        if i == nv - 1:
+                            prod[plane] = prod[plane] * value
             if sweep == SWEEPS - 1:
-                store(chunk).start()
+                for copy in store(chunk):
+                    copy.start()
             return packed
 
+        if sweep == SWEEPS - 1:
+            loads[10].wait()
         packed = lax.fori_loop(0, chunks, finish, jnp.zeros((cy, LANES), F32))
         if sweep < SWEEPS - 1:
             wall_out[sweep + 1] = packed
             start_halos(sweep + 1)
 
     for chunk in range(chunks):
-        store(chunk).wait()
+        for copy in store(chunk):
+            copy.wait()
     for peer in peers:
         cell_copy(peer, si).wait_send()
     for sweep in range(SWEEPS):
@@ -366,11 +374,14 @@
         hbm = pl.BlockSpec(memory_space=pltpu.HBM)
         dma = pltpu.SemaphoreType.DMA
         field = (nv, cx, cy, cz)
-        adjoint = pl.pallas_call(
+        return pl.pallas_call(
             functools.partial(kernel, n_chord, n_span, n_wall, nv, cx, cy, slots),
-            out_shape=jax.ShapeDtypeStruct(field, F32),
-            in_specs=[hbm] * 10,
-            out_specs=hbm,
+            out_shape=(
+                jax.ShapeDtypeStruct(field, F32),
+                jax.ShapeDtypeStruct((cx, cy, cz), F32),
+            ),
+            in_specs=[hbm] * 11,
+            out_specs=(hbm, hbm),
             scratch_shapes=[
                 pltpu.SMEM(upper_blocks.shape, F32),
                 pltpu.SMEM(lower_blocks.shape, F32),
@@ -382,6 +393,7 @@
                 pltpu.VMEM(field, F32),
                 pltpu.VMEM(field, F32),
                 pltpu.VMEM((3, cx, cy, cz), F32),
+                pltpu.VMEM((cx, cy, cz), F32),
                 pltpu.VMEM((SWEEPS, nv, cx + 2, cy, cz), F32),
                 pltpu.VMEM(field, F32),
                 pltpu.VMEM((pairs, 2 * cx * cy, 2 * cz), BF16),
@@ -403,7 +415,8 @@
                 pltpu.VMEM((total, LANES), F32),
                 pltpu.VMEM((pairs, 2 * total, 2 * LANES), BF16),
                 pltpu.VMEM((pairs, LANES, 2 * LANES), F32),
-                dma((10,)),
+                dma((11,)),
+                dma((cx // STEP,)),
                 dma((cx // STEP,)),
                 dma((SWEEPS, 6)),
                 dma((SWEEPS, 6)),
@@ -422,9 +435,9 @@
             ),
         )(
             sensitivity, diagonal, face_coef, upper_blocks, lower_blocks,
-            iface_blocks.transpose(1, 0, 2), send_cell, target_cell, orient, iface_weight,
-        )
-        return adjoint, production * adjoint[nv - 1]
+            iface_blocks.transpose(1, 0, 2), production,
+            send_cell, target_cell, orient, iface_weight,
+        )
 
     grid = P(None, "chord", "span", "wall")
     rows = P("chord", "span", "wall", None, None)

time: 22.9 us -> 22 us (0.961)
  other arithmetic: 1.48 us -> 0 us
  local copies, waits for them, and re-layouts: 1.78 us -> 2.44 us
    mul x1 -> x0, other arithmetic: 1.48 us -> none  [local(): return (adjoint, production * adjoint[nv - 1])]
    unnamed x3 -> x4, local copies, waits for them, and re-layouts: 1.78 us -> 2.44 us
where the time goes in v3:
time: 22 us; the launch traced here: 21.9 us
  Pallas kernels  18.8 us (85%)
  local copies, waits for them, and re-layouts  2.44 us (11%)
  between operations  0.65 us (3%)
    pallas_call x1, Pallas kernels, local(): pl.pallas_call(functools.partial(kernel, n_chord, n_span, n_wall, nv, cx,...  18.8 us
    unnamed x4, local copies, waits for them, and re-layouts  2.44 us

profile of v3, /device:TPU:0, one launch (start us, length us, event | category | flops | bytes accessed | tf_op | source)
XLA Modules:
  0.0 21.9 jit_solution(539422890345508810)
XLA Ops:
  0.6 18.8 %shard_map.122 = (f32[6,8,16,128]{3,2,1,0:T(8,128)}, f32[8,16,128]{2,1,0:T(8,128)}) custom-call(f32[6,8,16,128]{3,2,1,0:T(8,128)} %sens_hbm.1, f32[6,8,16,128]{3,2,1,0:T(8,128)} %diag_hbm.1, f32[3,8,16,128]{3,2,1,0:T(8,128)} %face_hbm.1, f32[3,6,6]{2,1,0:T(8,128)} %up_hbm.1, f32[3,6,6]{2,1,0:T(8,128)} %low_hbm.1, f32[6,2,6]{2,1,0:T(2,128)} %bitcast.1, ...), custom_call_target="tpu_custom_call" | custom-call | flops 21233664 | bytes 1507328 | tf_op jit(solution)/shard_map/pallas_call | solution.py:377
  19.4 0.0 copy-start
  19.4 1.8 %copy.15 = f32[6,8,16,128]{3,2,1,0:T(8,128)} copy(f32[6,8,16,128]{3,2,1,0:T(8,128)} %get-tuple-element.4) | data formatting | bytes 786432
  21.2 0.0 copy-done
  21.2 0.6 %copy.16 = f32[8,16,128]{2,1,0:T(8,128)} copy(f32[8,16,128]{2,1,0:T(8,128)S(1)} %copy-done) | data formatting | bytes 131072
Async XLA Ops:
  19.4 1.8 %copy-start = (f32[8,16,128]{2,1,0:T(8,128)S(1)}, f32[8,16,128]{2,1,0:T(8,128)}, u32[]{:S(2)}) copy-start(f32[8,16,128]{2,1,0:T(8,128)} %get-tuple-element.5) | copy-start | bytes 196612
